TPU v7x, 256 devices: a whole 4x4x8 slice. The times are simulated.
256 devices in a mesh: band: 64 (over y, z, core), lev: 4 (over x).
Axes of the slice: x: 4, y: 4, z: 8, core: 2. Of those that a mesh axis runs over, the one named last changes fastest.
Arguments:
- arrival_adj: bfloat16 [4, 16, 1280, 2560], P(None, None, ('band', 'lev')), may hold values from -6 to 6
- block_weights: bfloat16 [64, 4, 100, 128, 128], P('band', 'lev'), may hold values from -0.5 to 0.5
- dest_band: int32 [64, 4, 100], P('band', 'lev'), may hold values from 0 to 63, as said below
- dest_block: int32 [64, 4, 100], P('band', 'lev'), may hold values from 0 to 99, as said below
- lower_coef: float32 [4, 16], replicated, may hold values from 0.05 to 4
- upper_coef: float32 [4, 16], replicated, may hold values from 0.05 to 4
- order_pairs: int32 [64], replicated, may hold values from 0 to 63, each once
- legendre: bfloat16 [64, 1280, 1281], P('band'), may hold values from -0.15625 to 0.15625
Outputs:
- grid_adj: float32 [4, 16, 1280, 2560], P(None, None, ('band', 'lev'))
- spectral: float32 [64, 1281, 2, 64], P('band', None, None, 'lev')
Inputs may be any that keep to these rules, and one draw needn't show every extreme that they name: `dest_band`: A slot's target band lies within 2 bands of its own band; no device has more than 40 slots naming one band, and some device has exactly that many. In every latitude group, each column block of each band is named (by dest_band and dest_block together) by exactly one slot over all devices of the group. `order_pairs`: each pair slot names a different lower order; the pair stands for orders m and 1279 - m.
All inputs are finite; a program needn't handle non-finite values.
Results may differ from a plain program's by a relative error of at most 0.0041.
Values may be sent and summed in bfloat16 or wider, within the bound.
No kernel may reach another device: no remote copies, remote signals or barrier semaphores. Data moves between devices by JAX's collectives and lax.ppermute only.
A program may use at most 128 MiB of HBM per device.

v0:
```python
import math

import jax
import jax.numpy as jnp
from jax import lax
from jax.experimental import pallas as pl
from jax.experimental.pallas import tpu as pltpu
from jax.sharding import PartitionSpec as P

FIELDS = 4
LEVELS = 16
FEATURES = 64
LONGITUDES = 2560
ORDERS = 1280
LAT_DEV = 5
BANDS = 64
GROUPS = 4
CHIPS = 32
REACH = 5
CAP = 40
BLOCK = 128
PACK = CAP * FEATURES + 16
UNROLL = 10
SLOTS = 100
COL_BLOCKS = 20
LATITUDES = 1280
MIB = 1 << 20
F32 = jnp.float32
BF16 = jnp.bfloat16
VMEM = pl.BlockSpec(memory_space=pltpu.VMEM)
SMEM = pl.BlockSpec(memory_space=pltpu.SMEM)
HBM = pl.BlockSpec(memory_space=pl.ANY)


def iota(shape, dim):
    return lax.broadcasted_iota(jnp.int32, shape, dim)


def turned(steps):
    steps = steps - LONGITUDES * jnp.floor((steps + 0.5) * (1.0 / LONGITUDES))
    away = jnp.abs(steps - ORDERS)
    near = jnp.minimum(away, ORDERS - away)
    angle = near * (math.pi / ORDERS)
    t = angle * angle
    value = -1.0 / 87178291200.0
    for term in (479001600.0, -3628800.0, 40320.0, -720.0, 24.0, -2.0, 1.0):
        value = value * t + 1.0 / term
    return jnp.where(away > ORDERS // 2, value, -value)


def solve_rows(below, diagonal, above, start):
    ratios, values = [], []
    for k in range(LEVELS):
        if k == 0:
            inverse = 1.0 / diagonal[0]
            values.append(start[0] * inverse)
        else:
            inverse = 1.0 / (diagonal[k] - below[k] * ratios[k - 1])
            values.append((start[k] - below[k] * values[k - 1]) * inverse)
        ratios.append(above[k] * inverse if k < LEVELS - 1 else None)
    for k in range(LEVELS - 2, -1, -1):
        values[k] = values[k] - ratios[k] * values[k + 1]
    return values


def table_columns(orders, core):
    lane = iota((8, 2 * BLOCK), 1)
    within = lane & (BLOCK - 1)
    slot = (within & 31) * 2 + jnp.where(lane < BLOCK, core, 1 - core)
    order = jnp.zeros((8, 2 * BLOCK), jnp.int32)
    for p in range(BANDS):
        order = jnp.where(slot == p, orders[p], order)
    order = jnp.where((within & 32) == 0, order, ORDERS - 1 - order).astype(F32)
    quarter = jnp.where((within & 64) == 0, 0.0, float(LONGITUDES // 4))
    return order[0:1], quarter[0:1]


def write_table(order, quarter, table_ref):
    inner = iota((BLOCK, 2 * BLOCK), 0).astype(F32) * order
    cos_in = turned(inner)
    sin_in = turned(inner + 3.0 * (LONGITUDES // 4))
    scale = 1.0 / math.sqrt(LONGITUDES)
    outer = iota((24, 2 * BLOCK), 0).astype(F32) * (BLOCK * order) + quarter
    cos_out = turned(outer) * scale
    sin_out = turned(outer + 3.0 * (LONGITUDES // 4)) * scale
    for block in range(COL_BLOCKS):
        full = cos_out[block : block + 1] * cos_in - sin_out[block : block + 1] * sin_in
        head = full.astype(BF16)
        table_ref[block, 0:BLOCK, :] = head
        table_ref[block, BLOCK:, :] = (full - head.astype(F32)).astype(BF16)


def solve_kernel(lower_ref, upper_ref, lifts, lift_ref, work):
    lower, upper = lower_ref[...], upper_ref[...]
    lows = [jnp.broadcast_to(lower[:, k : k + 1], (FIELDS, BLOCK)) for k in range(LEVELS)]
    ups = [jnp.broadcast_to(upper[:, k : k + 1], (FIELDS, BLOCK)) for k in range(LEVELS)]
    diagonal = [1.0 + lows[k] + ups[k] for k in range(LEVELS)]
    col = iota((FIELDS, BLOCK), 1)
    mine = ((col >> 4) & 3) == iota((FIELDS, BLOCK), 0)
    zero = jnp.zeros((FIELDS, BLOCK), F32)
    unit = [jnp.where((col & 15) == k, 1.0, 0.0) for k in range(LEVELS)]
    shift_down = [zero] + [-ups[k - 1] for k in range(1, LEVELS)]
    shift_up = [-lows[k + 1] for k in range(LEVELS - 1)] + [zero]
    rows = solve_rows(shift_down, diagonal, shift_up, unit)
    for k in range(LEVELS):
        work[pl.ds(k, FIELDS, stride=LEVELS), :] = jnp.where(mine, rows[k], 0.0)
    full = work[...]
    head = full.astype(BF16).astype(F32)
    lift_ref[...] = jnp.where(iota((FEATURES, BLOCK), 1) < FEATURES, head, full - head).astype(BF16)
    plain_down = [zero] + [-lows[k] for k in range(1, LEVELS)]
    plain_up = [-ups[k] for k in range(LEVELS - 1)] + [zero]
    rows = solve_rows(plain_down, diagonal, plain_up, unit)
    for k in range(LEVELS):
        work[pl.ds(k, FIELDS, stride=LEVELS), :] = rows[k]
    wide = jnp.concatenate([work[...]] * FIELDS, axis=1)
    row = iota(wide.shape, 0)
    lane = iota(wide.shape, 1)
    owned = (row >> 4) == (lane >> 7)
    for q in range(8):
        full = jnp.where(owned & (((lane & 127) >> 4) == q), wide, 0.0)
        head = full.astype(BF16)
        lifts[q, 0:64] = head
        lifts[q, 64:128] = head
        lifts[q, 128:192] = (full - head.astype(F32)).astype(BF16)
        lifts[q, 192:256] = jnp.zeros_like(head)


def block_row(block):
    return (
        (block >= 20).astype(jnp.int32)
        + (block >= 40).astype(jnp.int32)
        + (block >= 60).astype(jnp.int32)
        + (block >= 80).astype(jnp.int32)
    )


def payload_kernel(
    dest_band, dest_block, orders, arrival_in, weights_in,
    own_part, other_part, kept, pair_out, near_out, up_out, down_out,
    arrival, weights, table, packs, tags, counts, places, in_sems, out_sems,
):
    band = lax.axis_index("band")
    core = lax.rem(band, 2)
    loads = [pltpu.make_async_copy(arrival_in, arrival, in_sems.at[LAT_DEV])]
    for lat in range(LAT_DEV):
        part = pl.ds(lat * COL_BLOCKS, COL_BLOCKS)
        loads.append(
            pltpu.make_async_copy(weights_in.at[part], weights.at[part], in_sems.at[lat])
        )
    for load in loads:
        load.start()
    for g in range(REACH):
        counts[g] = 0
    tags[...] = jnp.zeros_like(tags)
    own_part[...] = jnp.zeros_like(own_part)
    other_part[...] = jnp.zeros_like(other_part)
    write_table(*table_columns(orders, core), table)
    lane = iota((16, BLOCK), 1)

    def weigh(col, lat):
        j = lat * COL_BLOCKS + col
        rows = arrival[:, lat, :, pl.ds(pl.multiple_of(col * BLOCK, BLOCK), BLOCK)]
        payload = jnp.dot(
            rows.reshape(FEATURES, BLOCK), weights[j], preferred_element_type=F32
        ).astype(BF16)
        g = dest_band[j] - band + 2
        rank = counts[g]
        counts[g] = rank + 1
        start = pl.multiple_of(g * PACK + rank * FEATURES, 16)
        places[j] = start
        packs[pl.ds(start, FEATURES), :] = payload
        tag = (dest_block[j] + 1).astype(F32)
        tags[g] = jnp.where(lane == rank, tag, tags[g])
        return lat

    loads[0].wait()
    for lat in range(LAT_DEV):
        loads[1 + lat].wait()
        lax.fori_loop(0, COL_BLOCKS, weigh, lat, unroll=UNROLL)
    for g in range(REACH):
        packs[g * PACK + CAP * FEATURES : (g + 1) * PACK, :] = tags[g].astype(BF16)

    def ship(group, out, n):
        source = packs.at[pl.ds(pl.multiple_of(group * PACK, 16), PACK)]
        return pltpu.make_async_copy(source, out, out_sems.at[n])

    shipped = [
        ship(2, kept, 0),
        ship(3 - 2 * core, pair_out, 1),
        ship(1 + 2 * core, near_out, 2),
        ship(4, up_out, 3),
        ship(0, down_out, 4),
    ]
    for copy in shipped:
        copy.start()

    def analyse(j, carry):
        payload = packs[pl.ds(pl.multiple_of(places[j], 16), FEATURES), :]
        block = dest_block[j]
        lat = block_row(block)
        at = (dest_band[j] - band + 2) * LAT_DEV + lat
        col = block - lat * COL_BLOCKS
        twice = jnp.concatenate([payload, payload], axis=1)
        part = jnp.dot(twice, table[col], preferred_element_type=F32)
        own_part[at] = own_part[at] + part[:, :BLOCK]
        other_part[at] = other_part[at] + part[:, BLOCK:]
        return carry

    lax.fori_loop(0, SLOTS, analyse, 0, unroll=UNROLL)
    for copy in shipped:
        copy.wait()


def spread_kernel(own, other, lifts, out, turned_rows, work):
    core = lax.rem(lax.axis_index("band"), 2)
    for near in range(6):
        for i in range(LAT_DEV):
            if near == 0:
                total = jnp.where(core == 0, own[i], other[i])
            elif near == 5:
                total = jnp.where(core == 1, own[20 + i], other[20 + i])
            else:
                total = own[(near - core) * LAT_DEV + i] + other[(near - 1 + core) * LAT_DEV + i]
            head = total.astype(BF16).astype(F32)
            flipped = jnp.concatenate([head, total - head], axis=0).T.astype(BF16)
            at = (near // 2) * LAT_DEV + i
            for q in range(4):
                turned_rows[(near % 2) * 4 + q, at * 32 : (at + 1) * 32, :] = flipped[
                    q * 32 : (q + 1) * 32
                ]
    for chunk in range(5):
        total = jnp.zeros((96, 4 * BLOCK), F32)
        for q in range(8):
            part = turned_rows[q, chunk * 96 : (chunk + 1) * 96, :]
            total = total + jnp.dot(
                jnp.concatenate([part, part], axis=1), lifts[q], preferred_element_type=F32
            )
        for r in range(3):
            for g in range(GROUPS):
                work[pl.ds(g * 16 + chunk * 3 + r, 32, stride=64), :] = total[
                    r * 32 : (r + 1) * 32, g * BLOCK : (g + 1) * BLOCK
                ]
    for g in range(GROUPS):
        work[pl.ds(g * 16 + 15, 32, stride=64), :] = jnp.zeros((32, BLOCK), F32)
    out[...] = work[...].astype(BF16).reshape(out.shape)


def legendre_kernel(orders, parts, legendre, out, work, gathered):
    first = ORDERS - orders[lax.axis_index("band")]
    work[...] = parts[...].astype(F32).reshape(work.shape)
    for chip in range(CHIPS):
        for s in range(GROUPS):
            base = (chip * GROUPS + s) * 16
            total = work[base + 5 : base + 10, :]
            if chip > 0:
                total = total + work[base - 64 + 10 : base - 64 + 15, :]
            if chip < CHIPS - 1:
                total = total + work[base + 64 : base + 64 + 5, :]
            at = chip * 40 + s * LAT_DEV
            gathered[at : at + LAT_DEV, :] = total
            gathered[at + 20 : at + 20 + LAT_DEV, :] = pltpu.roll(total, 64, 1)
    right = gathered[...].astype(BF16)
    step = 256
    for low in range(0, ORDERS + 1, step):
        size = min(step, ORDERS + 1 - low)
        mixed = jnp.dot(legendre[low : low + size, :], right, preferred_element_type=F32).T
        degree = low + iota((16, size), 1)
        for r in range(2):
            picked = jnp.where(
                degree < first, mixed[r * 32 : r * 32 + 16], mixed[r * 32 + 16 : r * 32 + 32]
            )
            out[r, :, low : low + size] = picked


def grid_kernel(lift, *refs):
    sources = refs[:REACH]
    out, packs, work, tag_rows, tags, found, in_sems, tag_sem, out_sems = refs[REACH:]
    loads = [
        pltpu.make_async_copy(
            source, packs.at[pl.ds(n * PACK, PACK)], in_sems.at[n]
        )
        for n, source in enumerate(sources)
    ]
    for load in loads:
        load.start()
    for load in loads:
        load.wait()
    for n in range(REACH):
        row = packs[n * PACK + CAP * FEATURES : (n + 1) * PACK, :]
        tag_rows[n : n + 1, :] = row.astype(F32)[0:1].astype(jnp.int32)
    copy = pltpu.make_async_copy(tag_rows, tags, tag_sem)
    copy.start()
    copy.wait()

    for n in range(REACH):

        def note(r, carry):
            found[tags[n, r]] = n * PACK + r * FEATURES
            return carry

        lax.fori_loop(0, CAP, note, 0, unroll=8)
    head = lift[...]
    copies = []
    for lat in range(LAT_DEV):
        for col in range(0, COL_BLOCKS, 2):
            tag = lat * COL_BLOCKS + col + 1
            rows = jnp.concatenate(
                [
                    packs[pl.ds(pl.multiple_of(found[tag + n], 16), FEATURES), :]
                    for n in range(2)
                ],
                axis=1,
            )
            value = jnp.dot(
                head, jnp.concatenate([rows, rows], axis=0), preferred_element_type=F32
            )
            work[:, lat, :, col * BLOCK : (col + 2) * BLOCK] = value.reshape(
                FIELDS, LEVELS, 2 * BLOCK
            )
        copies.append(
            pltpu.make_async_copy(work.at[:, lat], out.at[:, lat], out_sems.at[lat])
        )
        copies[-1].start()
    for copy in copies:
        copy.wait()


def call(kernel, ins, outs, shapes, scratch, name, flops, limit=16):
    return pl.pallas_call(
        kernel,
        in_specs=ins,
        out_specs=outs,
        out_shape=[jax.ShapeDtypeStruct(s, d) for s, d in shapes],
        scratch_shapes=scratch,
        name=name,
        cost_estimate=pl.CostEstimate(flops=flops, bytes_accessed=4 * MIB, transcendentals=0),
        compiler_params=pltpu.CompilerParams(vmem_limit_bytes=limit * MIB),
    )


def on_device(
    arrival_adj, block_weights, dest_band, dest_block, lower_coef, upper_coef, order_pairs, legendre
):
    arrival = arrival_adj.transpose(0, 2, 1, 3)
    weights = block_weights.reshape(SLOTS, BLOCK, BLOCK)
    targets = dest_band.reshape(SLOTS)
    blocks = dest_block.reshape(SLOTS)
    part_shape = ((REACH * LAT_DEV, FEATURES, BLOCK), F32)
    pack_shape = ((PACK, BLOCK), BF16)
    own, other, kept, pair, near, up, down = call(
        payload_kernel,
        [SMEM, SMEM, SMEM, HBM, HBM],
        [VMEM, VMEM] + [HBM] * 5,
        [part_shape] * 2 + [pack_shape] * 5,
        [
            pltpu.VMEM((FIELDS, LAT_DEV, LEVELS, LONGITUDES), BF16),
            pltpu.VMEM((SLOTS, BLOCK, BLOCK), BF16),
            pltpu.VMEM((COL_BLOCKS, 2 * BLOCK, 2 * BLOCK), BF16),
            pltpu.VMEM((REACH * PACK, BLOCK), BF16),
            pltpu.VMEM((REACH, 16, BLOCK), F32),
            pltpu.SMEM((8,), jnp.int32),
            pltpu.SMEM((SLOTS,), jnp.int32),
            pltpu.SemaphoreType.DMA((LAT_DEV + 1,)),
            pltpu.SemaphoreType.DMA((5,)),
        ],
        "payload_and_part_fourier",
        3 * 10**9,
        56,
    )(targets, blocks, order_pairs, arrival, weights)
    lifts, lift = call(
        solve_kernel,
        [VMEM, VMEM],
        [VMEM] * 2,
        [((8, 2 * BLOCK, 4 * BLOCK), BF16), ((FEATURES, BLOCK), BF16)],
        [pltpu.VMEM((FEATURES, BLOCK), F32)],
        "inverse_of_vertical_operator",
        10**9,
    )(lower_coef, upper_coef)

    swap = [(b, b ^ 1) for b in range(BANDS)]
    hop = [(b, b + 1) for b in range(1, BANDS - 1, 2)] + [(b, b - 1) for b in range(2, BANDS, 2)]
    rise = [(b, b + 2) for b in range(BANDS - 2)]
    fall = [(b, b - 2) for b in range(2, BANDS)]
    other = lax.ppermute(other, "band", swap)
    (message,) = call(
        spread_kernel,
        [VMEM] * 3,
        [VMEM],
        [((CHIPS * GROUPS, 16, BLOCK), BF16)],
        [
            pltpu.VMEM((8, 480, BLOCK), BF16),
            pltpu.VMEM((CHIPS * GROUPS * 16, BLOCK), F32),
        ],
        "vertical_solve_of_fourier",
        10**9,
    )(own, other, lifts)
    same_core = [
        [(chip * 2 + core) * GROUPS + s for chip in range(CHIPS) for s in range(GROUPS)]
        for core in range(2)
    ]
    parts = lax.all_to_all(
        message, ("band", "lev"), split_axis=0, concat_axis=0, axis_index_groups=same_core, tiled=True
    )
    received = [
        kept,
        lax.ppermute(pair, "band", swap),
        lax.ppermute(near, "band", hop),
        lax.ppermute(up, "band", rise),
        lax.ppermute(down, "band", fall),
    ]
    (grid_adj,) = call(
        grid_kernel,
        [VMEM] + [HBM] * REACH,
        [HBM],
        [((FIELDS, LAT_DEV, LEVELS, LONGITUDES), F32)],
        [
            pltpu.VMEM((REACH * PACK, BLOCK), BF16),
            pltpu.VMEM((FIELDS, LAT_DEV, LEVELS, LONGITUDES), F32),
            pltpu.VMEM((8, BLOCK), jnp.int32),
            pltpu.SMEM((8, BLOCK), jnp.int32),
            pltpu.SMEM((SLOTS + 1,), jnp.int32),
            pltpu.SemaphoreType.DMA((REACH,)),
            pltpu.SemaphoreType.DMA,
            pltpu.SemaphoreType.DMA((LAT_DEV,)),
        ],
        "grid_vertical_solve",
        2 * 10**9,
    )(lift, *received)
    (spectral,) = call(
        legendre_kernel,
        [SMEM, VMEM, VMEM],
        [VMEM],
        [((2, LEVELS, ORDERS + 1), F32)],
        [
            pltpu.VMEM((CHIPS * GROUPS * 16, BLOCK), F32),
            pltpu.VMEM((LATITUDES, BLOCK), F32),
        ],
        "legendre_analysis",
        2 * 10**9,
    )(order_pairs, parts, legendre[0].T)
    return (grid_adj.transpose(0, 2, 1, 3), spectral.transpose(2, 0, 1)[None])


def solution(mesh):
    in_specs = (
        P(None, None, ("band", "lev"), None),
        P("band", "lev", None, None, None),
        P("band", "lev", None),
        P("band", "lev", None),
        P(),
        P(),
        P(),
        P("band", None, None),
    )
    out_specs = (P(None, None, ("band", "lev"), None), P("band", None, None, "lev"))
    return jax.shard_map(
        on_device, mesh=mesh, in_specs=in_specs, out_specs=out_specs, check_vma=False
    )
```

profile of v0, /device:TPU:25, one launch (start us, length us, event | category | flops | bytes accessed | tf_op | source)
XLA Modules:
  0.0 76.2 jit_solution(16728205601135090059)
XLA Ops:
  0.6 0.0 copy-start.2
  0.6 0.0 copy-start.3
  0.7 9.6 %payload_and_part_fourier.1 = (f32[25,64,128]{2,1,0:T(8,128)}, f32[25,64,128]{2,1,0:T(8,128)}, bf16[2576,128]{1,0:T(8,128)(2,1)}, bf16[2576,128]{1,0:T(8,128)(2,...) custom-call(s32[100]{0:T(128)} %bitcast.14, s32[100]{0:T(128)} %bitcast.15, ...), custom_call_target="tpu_custom_call" | custom-call | flops 3000000000 | bytes 4194304 | tf_op jit(solution)/shard_map/payload_and_part_fourier/pallas_call | solution.py:350
  10.3 0.0 copy-start
  10.3 0.8 %collective-permute-start.4 = (f32[25,64,128]{2,1,0:T(8,128)}, f32[25,64,128]{2,1,0:T(8,128)S(1)}, u32[]{:S(2)}, u32[]{:S(2)}) collective-permute-start(f32[25,64,128]{2,1,0:T(8,128)} %get-tuple-element.18), channel_id=1, source_target_pairs={{0,4},{4,0},{8,12},{12,8},{16,20},{20,16},{24,28},{28,24},{32,36},... | collective-permute-start | bytes 2457608 | tf_op jit(solution)/shard_map/ppermute | solution.py:384
  11.1 0.5 inverse_of_vertical_operator.1
  11.6 1.6 %collective-permute-done.4.other = f32[25,64,128]{2,1,0:T(8,128)S(1)} collective-permute-done((f32[25,64,128]{2,1,0:T(8,128)}, f32[25,64,128]{2,1,0:T(8,128)S(1)}, u32[]{:S(2)}, u32[]{:S(2)}) %collective-permute-start.4) | collective-permute-done | bytes 819232 | tf_op jit(solution)/shard_map/ppermute | solution.py:384
  13.2 3.5 %vertical_solve_of_fourier.1 = bf16[128,16,128]{2,1,0:T(8,128)(2,1)} custom-call(f32[25,64,128]{2,1,0:T(8,128)S(1)} %copy-done, f32[25,64,128]{2,1,0:T(8,128)S(1)} %collective-permute-done.4.other, bf16[8,256,512]{2,1,0:T(8,128)(2,1)S(1)} %get-tuple-element.19.lifts), custom_call_target="tpu_custom_call" | custom-call | flops 1000000000 | bytes 4194304 | tf_op jit(solution)/shard_map/vertical_solve_of_fourier/pallas_call | solution.py:385
  16.7 15.1 %all-to-all-start = ((bf16[128,16,128]{2,1,0:T(8,128)(2,1)}), bf16[128,16,128]{2,1,0:T(8,128)(2,1)S(1)}, u32[]{:S(2)}, u32[]{:S(2)}) async-start(bf16[128,16,128]{2,1,0:T(8,128)(2,1)} %vertical_solve_of_fourier.1), calls=%async_computation | async-start | bytes 1048576 | tf_op jit(solution)/shard_map/all_to_all | solution.py:401
  31.8 1.0 %collective-permute-start = (bf16[2576,128]{1,0:T(8,128)(2,1)}, bf16[2576,128]{1,0:T(8,128)(2,1)S(1)}, u32[]{:S(2)}, u32[]{:S(2)}) collective-permute-start(bf16[2576,128]{1,0:T(8,128)(2,1)} %get-tuple-element.13), channel_id=1, source_target_pairs={{0,4},{4,0},{8,12},{12,8},{16,20},{20,16},{24,28},{28,24},{32,36},... | collective-permute-start | bytes 1978376 | tf_op jit(solution)/shard_map/ppermute | solution.py:406
  32.8 0.0 copy-done.8
  32.8 3.0 %collective-permute-start.1 = (bf16[2576,128]{1,0:T(8,128)(2,1)S(1)}, bf16[2576,128]{1,0:T(8,128)(2,1)S(1)}, u32[]{:S(2)}, u32[]{:S(2)}) collective-permute-start(bf16[2576,128]{1,0:T(8,128)(2,1)S(1)} %copy-done.8), channel_id=1, source_target_pairs={{4,8},{12,16},{20,24},{28,32},{36,40},{44,48},{52,56},{60,64},{68,... | collective-permute-start | bytes 1978376 | tf_op jit(solution)/shard_map/ppermute | solution.py:407
  35.9 3.1 %collective-permute-start.2 = (bf16[2576,128]{1,0:T(8,128)(2,1)S(1)}, bf16[2576,128]{1,0:T(8,128)(2,1)S(1)}, u32[]{:S(2)}, u32[]{:S(2)}) collective-permute-start(bf16[2576,128]{1,0:T(8,128)(2,1)S(1)} %copy-done.7), channel_id=1, source_target_pairs={{0,8},{4,12},{8,16},{12,20},{16,24},{20,28},{24,32},{28,36},{32,40... | collective-permute-start | bytes 1978376 | tf_op jit(solution)/shard_map/ppermute | solution.py:408
  39.0 4.3 %collective-permute-start.3 = (bf16[2576,128]{1,0:T(8,128)(2,1)S(1)}, bf16[2576,128]{1,0:T(8,128)(2,1)S(1)}, u32[]{:S(2)}, u32[]{:S(2)}) collective-permute-start(bf16[2576,128]{1,0:T(8,128)(2,1)S(1)} %copy-done.6), channel_id=1, source_target_pairs={{8,0},{12,4},{16,8},{20,12},{24,16},{28,20},{32,24},{36,28},{40,32... | collective-permute-start | bytes 1978376 | tf_op jit(solution)/shard_map/ppermute | solution.py:409
  43.3 0.0 collective-permute-done.refs_1_
  43.3 15.7 %collective-permute-done.1.refs_2_ = bf16[2576,128]{1,0:T(8,128)(2,1)S(1)} collective-permute-done((bf16[2576,128]{1,0:T(8,128)(2,1)S(1)}, bf16[2576,128]{1,0:T(8,128)(2,1)S(1)}, u32[]{:S(2)}, u32[]{:S(2)}) %collective-permute-start.1) | collective-permute-done | bytes 659488 | tf_op jit(solution)/shard_map/ppermute | solution.py:407
  59.0 8.4 %collective-permute-done.2.refs_3_ = bf16[2576,128]{1,0:T(8,128)(2,1)S(1)} collective-permute-done((bf16[2576,128]{1,0:T(8,128)(2,1)S(1)}, bf16[2576,128]{1,0:T(8,128)(2,1)S(1)}, u32[]{:S(2)}, u32[]{:S(2)}) %collective-permute-start.2) | collective-permute-done | bytes 659488 | tf_op jit(solution)/shard_map/ppermute | solution.py:408
  67.4 0.0 collective-permute-done.3.refs_4_
  67.4 0.0 copy-done.5
  67.4 4.3 %grid_vertical_solve.1 = f32[4,5,16,2560]{3,2,1,0:T(8,128)} custom-call(bf16[64,128]{1,0:T(8,128)(2,1)S(1)} %get-tuple-element.11.lift, bf16[2576,128]{1,0:T(8,128)(2,1)S(1)} %copy-done.5, bf16[2576,128]{1,0:T(8,128)(2,1)S(1)} %collective-permute-done.refs_1_, bf16[2576,128]{1,0:T(8,128)(2,1)S(1)} %collective-permute-done.1.refs_2_, ...), custom_call_target="tpu_custom_call" | custom-call | flops 2000000000 | bytes 4194304 | tf_op jit(solution)/shard_map/grid_vertical_solve/pallas_call | solution.py:411
  71.7 0.0 all-to-all-done.parts
  71.7 0.0 copy-start.1
  71.8 1.9 %copy-done.1 = bf16[1,1280,1281]{1,2,0:T(8,128)(2,1)S(1)} copy-done((bf16[1,1280,1281]{1,2,0:T(8,128)(2,1)S(1)}, bf16[1,1280,1281]{1,2,0:T(8,128)(2,1)}, u32[]{:S(2)}) %copy-start.1) | copy-done | bytes 3279384
  73.7 2.5 %legendre_analysis.1 = f32[2,16,1281]{2,1,0:T(8,128)} custom-call(s32[64]{0:T(128)S(1)} %copy-done.4, bf16[128,16,128]{2,1,0:T(8,128)(2,1)S(1)} %all-to-all-done.parts, bf16[1281,1280]{1,0:T(8,128)(2,1)S(1)} %bitcast.11), custom_call_target="tpu_custom_call" | custom-call | flops 2000000000 | bytes 4194304 | tf_op jit(solution)/shard_map/legendre_analysis/pallas_call | solution.py:429
  (11 shorter events, 0.0 us)
Async XLA Ops:
  0.6 10.4 %copy-start.2 = (f32[4,16]{1,0:T(4,128)S(1)}, f32[4,16]{1,0:T(4,128)}, u32[]{:S(2)}) copy-start(f32[4,16]{1,0:T(4,128)} %lower_ref.1) | copy-start | bytes 772
  0.6 10.4 %copy-start.3 = (f32[4,16]{1,0:T(4,128)S(1)}, f32[4,16]{1,0:T(4,128)}, u32[]{:S(2)}) copy-start(f32[4,16]{1,0:T(4,128)} %upper_ref.1) | copy-start | bytes 772
  10.3 3.0 %copy-start = (f32[25,64,128]{2,1,0:T(8,128)S(1)}, f32[25,64,128]{2,1,0:T(8,128)}, u32[]{:S(2)}) copy-start(f32[25,64,128]{2,1,0:T(8,128)} %get-tuple-element.17.own) | copy-start | bytes 2457604
  10.3 2.9 %collective-permute-start.4 = (f32[25,64,128]{2,1,0:T(8,128)}, f32[25,64,128]{2,1,0:T(8,128)S(1)}, u32[]{:S(2)}, u32[]{:S(2)}) collective-permute-start(f32[25,64,128]{2,1,0:T(8,128)} %get-tuple-element.18), channel_id=1, source_target_pairs={{0,4},{4,0},{8,12},{12,8},{16,20},{20,16},{24,28},{28,24},{32,36},... | collective-permute-start | bytes 2457608 | tf_op jit(solution)/shard_map/ppermute | solution.py:384
  11.6 21.3 %copy-start.8 = (bf16[2576,128]{1,0:T(8,128)(2,1)S(1)}, bf16[2576,128]{1,0:T(8,128)(2,1)}, u32[]{:S(2)}) copy-start(bf16[2576,128]{1,0:T(8,128)(2,1)} %get-tuple-element.14) | copy-start | bytes 1978372
  11.6 24.3 %copy-start.7 = (bf16[2576,128]{1,0:T(8,128)(2,1)S(1)}, bf16[2576,128]{1,0:T(8,128)(2,1)}, u32[]{:S(2)}) copy-start(bf16[2576,128]{1,0:T(8,128)(2,1)} %get-tuple-element.15) | copy-start | bytes 1978372
  11.6 27.4 %copy-start.6 = (bf16[2576,128]{1,0:T(8,128)(2,1)S(1)}, bf16[2576,128]{1,0:T(8,128)(2,1)}, u32[]{:S(2)}) copy-start(bf16[2576,128]{1,0:T(8,128)(2,1)} %get-tuple-element.16) | copy-start | bytes 1978372
  11.6 55.8 %copy-start.5 = (bf16[2576,128]{1,0:T(8,128)(2,1)S(1)}, bf16[2576,128]{1,0:T(8,128)(2,1)}, u32[]{:S(2)}) copy-start(bf16[2576,128]{1,0:T(8,128)(2,1)} %get-tuple-element.12.refs_0_) | copy-start | bytes 1978372
  16.7 55.0 %all-to-all-start = ((bf16[128,16,128]{2,1,0:T(8,128)(2,1)}), bf16[128,16,128]{2,1,0:T(8,128)(2,1)S(1)}, u32[]{:S(2)}, u32[]{:S(2)}) async-start(bf16[128,16,128]{2,1,0:T(8,128)(2,1)} %vertical_solve_of_fourier.1), calls=%async_computation | async-start | bytes 1048576 | tf_op jit(solution)/shard_map/all_to_all | solution.py:401
  31.8 11.5 %collective-permute-start = (bf16[2576,128]{1,0:T(8,128)(2,1)}, bf16[2576,128]{1,0:T(8,128)(2,1)S(1)}, u32[]{:S(2)}, u32[]{:S(2)}) collective-permute-start(bf16[2576,128]{1,0:T(8,128)(2,1)} %get-tuple-element.13), channel_id=1, source_target_pairs={{0,4},{4,0},{8,12},{12,8},{16,20},{20,16},{24,28},{28,24},{32,36},... | collective-permute-start | bytes 1978376 | tf_op jit(solution)/shard_map/ppermute | solution.py:406
  32.8 26.1 %collective-permute-start.1 = (bf16[2576,128]{1,0:T(8,128)(2,1)S(1)}, bf16[2576,128]{1,0:T(8,128)(2,1)S(1)}, u32[]{:S(2)}, u32[]{:S(2)}) collective-permute-start(bf16[2576,128]{1,0:T(8,128)(2,1)S(1)} %copy-done.8), channel_id=1, source_target_pairs={{4,8},{12,16},{20,24},{28,32},{36,40},{44,48},{52,56},{60,64},{68,... | collective-permute-start | bytes 1978376 | tf_op jit(solution)/shard_map/ppermute | solution.py:407
  35.9 31.5 %collective-permute-start.2 = (bf16[2576,128]{1,0:T(8,128)(2,1)S(1)}, bf16[2576,128]{1,0:T(8,128)(2,1)S(1)}, u32[]{:S(2)}, u32[]{:S(2)}) collective-permute-start(bf16[2576,128]{1,0:T(8,128)(2,1)S(1)} %copy-done.7), channel_id=1, source_target_pairs={{0,8},{4,12},{8,16},{12,20},{16,24},{20,28},{24,32},{28,36},{32,40... | collective-permute-start | bytes 1978376 | tf_op jit(solution)/shard_map/ppermute | solution.py:408
  39.0 28.4 %collective-permute-start.3 = (bf16[2576,128]{1,0:T(8,128)(2,1)S(1)}, bf16[2576,128]{1,0:T(8,128)(2,1)S(1)}, u32[]{:S(2)}, u32[]{:S(2)}) collective-permute-start(bf16[2576,128]{1,0:T(8,128)(2,1)S(1)} %copy-done.6), channel_id=1, source_target_pairs={{8,0},{12,4},{16,8},{20,12},{24,16},{28,20},{32,24},{36,28},{40,32... | collective-permute-start | bytes 1978376 | tf_op jit(solution)/shard_map/ppermute | solution.py:409
  67.4 4.4 %copy-start.4 = (s32[64]{0:T(128)S(1)}, s32[64]{0:T(128)}, u32[]{:S(2)}) copy-start(s32[64]{0:T(128)} %orders.3) | copy-start | bytes 772
  71.7 1.9 %copy-start.1 = (bf16[1,1280,1281]{1,2,0:T(8,128)(2,1)S(1)}, bf16[1,1280,1281]{1,2,0:T(8,128)(2,1)}, u32[]{:S(2)}) copy-start(bf16[1,1280,1281]{1,2,0:T(8,128)(2,1)} %param.15) | copy-start | bytes 9838084
where the time goes:
time: 76.5 us; the launch traced here: 76.2 us
  starting transfers between devices  27.3 us (36%)
  waiting for transfers between devices  25.7 us (34%)
  Pallas kernels  20.5 us (27%)
  local copies, waits for them, and re-layouts  1.96 us (3%)
  between operations  0.8 us (1%)
    ppermute x1, waiting for transfers between devices, on_device(): lax.ppermute(near, 'band', hop)  15.7 us
    all_to_all x1, starting transfers between devices, on_device(): lax.all_to_all(message, ('band', 'lev'), split_axis=0, concat_axis=0, axi...  15.1 us
    pallas_call x1, Pallas kernels, on_device(): call(payload_kernel, [SMEM, SMEM, SMEM, HBM, HBM], [VMEM, VMEM] + [HBM] *...  9.63 us
    ppermute x1, waiting for transfers between devices, on_device(): lax.ppermute(up, 'band', rise)  8.4 us
    pallas_call x1, Pallas kernels, on_device(): call(grid_kernel, [VMEM] + [HBM] * REACH, [HBM], [((FIELDS, LAT_DEV, LEVE...  4.33 us
    ppermute x1, starting transfers between devices, on_device(): lax.ppermute(down, 'band', fall)  4.27 us
    pallas_call x1, Pallas kernels, on_device(): call(spread_kernel, [VMEM] * 3, [VMEM], [((CHIPS * GROUPS, 16, BLOCK), BF...  3.48 us
    ppermute x1, starting transfers between devices, on_device(): lax.ppermute(up, 'band', rise)  3.12 us
  transfers between devices with their start and end apart: 6, of which 3 were waited for; matrix products, arithmetic and copies ran while one was open for 0% of the time, Pallas kernels for 6%

commit v1 on v0

v1 whole, which is shorter than its diff:
```python
import functools
import math

import jax
import jax.numpy as jnp
from jax import lax
from jax.experimental import pallas as pl
from jax.experimental.pallas import tpu as pltpu
from jax.sharding import PartitionSpec as P

FIELDS = 4
LEVELS = 16
FEATURES = 64
LONGITUDES = 2560
ORDERS = 1280
LAT_DEV = 5
BANDS = 64
GROUPS = 4
CHIPS = 32
REACH = 5
CAP = 40
FAR = 20
BLOCK = 128
TAG_ROWS = 16
PACK = TAG_ROWS + CAP * FEATURES
UNROLL = 10
SLOTS = 100
COL_BLOCKS = 20
LATITUDES = 1280
MIB = 1 << 20
F32 = jnp.float32
BF16 = jnp.bfloat16
VMEM = pl.BlockSpec(memory_space=pltpu.VMEM)
SMEM = pl.BlockSpec(memory_space=pltpu.SMEM)
HBM = pl.BlockSpec(memory_space=pltpu.HBM)
ANY = pl.BlockSpec(memory_space=pl.ANY)


def iota(shape, dim):
    return lax.broadcasted_iota(jnp.int32, shape, dim)


def turned(steps):
    steps = steps - LONGITUDES * jnp.floor((steps + 0.5) * (1.0 / LONGITUDES))
    away = jnp.abs(steps - ORDERS)
    near = jnp.minimum(away, ORDERS - away)
    angle = near * (math.pi / ORDERS)
    t = angle * angle
    value = -1.0 / 87178291200.0
    for term in (479001600.0, -3628800.0, 40320.0, -720.0, 24.0, -2.0, 1.0):
        value = value * t + 1.0 / term
    return jnp.where(away > ORDERS // 2, value, -value)


def solve_rows(below, diagonal, above, start):
    ratios, values = [], []
    for k in range(LEVELS):
        if k == 0:
            inverse = 1.0 / diagonal[0]
            values.append(start[0] * inverse)
        else:
            inverse = 1.0 / (diagonal[k] - below[k] * ratios[k - 1])
            values.append((start[k] - below[k] * values[k - 1]) * inverse)
        ratios.append(above[k] * inverse if k < LEVELS - 1 else None)
    for k in range(LEVELS - 2, -1, -1):
        values[k] = values[k] - ratios[k] * values[k + 1]
    return values


def write_tables(orders, core, inner_table, angles):
    lane = iota((8, BLOCK), 1)
    slot = (lane & 31) * 2 + jnp.where(lane < 64, core, 1 - core)
    order = jnp.zeros((8, BLOCK), jnp.int32)
    for p in range(BANDS):
        order = jnp.where(slot == p, orders[p], order)
    order = jnp.where((lane & 32) == 0, order, ORDERS - 1 - order).astype(F32)[0:1]
    three_quarters = 3.0 * (LONGITUDES // 4)
    inner = iota((BLOCK, BLOCK), 0).astype(F32) * order
    for part, full in enumerate((turned(inner), turned(inner + three_quarters))):
        head = full.astype(BF16)
        cols = slice(part * BLOCK, (part + 1) * BLOCK)
        inner_table[0:BLOCK, cols] = head
        inner_table[BLOCK:, cols] = (full - head.astype(F32)).astype(BF16)
    scale = 1.0 / math.sqrt(LONGITUDES)
    outer = iota((24, BLOCK), 0).astype(F32) * (BLOCK * order)
    angles[0] = turned(outer) * scale
    angles[1] = turned(outer + three_quarters) * scale


def solve_kernel(lower_in, upper_in, sums, lifts, lift_ref, own_part, lower_ref, upper_ref, work, sems):
    loads = [
        pltpu.make_async_copy(lower_in, lower_ref, sems.at[0]),
        pltpu.make_async_copy(upper_in, upper_ref, sems.at[1]),
    ]
    for load in loads:
        load.start()
    half = iota((FEATURES, BLOCK), 1) < 64

    def split(at, carry):
        real = sums[at, :, :BLOCK]
        imaginary = sums[at, :, BLOCK:]
        own_part[at] = jnp.where(half, real, pltpu.roll(imaginary, 64, 1))
        return carry

    lax.fori_loop(0, REACH * LAT_DEV + 1, split, 0, unroll=13)
    for load in loads:
        load.wait()
    lower, upper = lower_ref[...], upper_ref[...]
    lows = [jnp.broadcast_to(lower[:, k : k + 1], (FIELDS, BLOCK)) for k in range(LEVELS)]
    ups = [jnp.broadcast_to(upper[:, k : k + 1], (FIELDS, BLOCK)) for k in range(LEVELS)]
    diagonal = [1.0 + lows[k] + ups[k] for k in range(LEVELS)]
    col = iota((FIELDS, BLOCK), 1)
    mine = ((col >> 4) & 3) == iota((FIELDS, BLOCK), 0)
    zero = jnp.zeros((FIELDS, BLOCK), F32)
    unit = [jnp.where((col & 15) == k, 1.0, 0.0) for k in range(LEVELS)]
    shift_down = [zero] + [-ups[k - 1] for k in range(1, LEVELS)]
    shift_up = [-lows[k + 1] for k in range(LEVELS - 1)] + [zero]
    rows = solve_rows(shift_down, diagonal, shift_up, unit)
    for k in range(LEVELS):
        work[pl.ds(k, FIELDS, stride=LEVELS), :] = jnp.where(mine, rows[k], 0.0)
    full = work[...]
    head = full.astype(BF16).astype(F32)
    lift_ref[...] = jnp.where(iota((FEATURES, BLOCK), 1) < FEATURES, head, full - head).astype(BF16)
    plain_down = [zero] + [-lows[k] for k in range(1, LEVELS)]
    plain_up = [-ups[k] for k in range(LEVELS - 1)] + [zero]
    rows = solve_rows(plain_down, diagonal, plain_up, unit)
    for k in range(LEVELS):
        work[pl.ds(k, FIELDS, stride=LEVELS), :] = rows[k]
    wide = jnp.concatenate([work[...]] * FIELDS, axis=1)
    owned = (iota(wide.shape, 0) >> 4) == (iota(wide.shape, 1) >> 7)
    full = jnp.where(owned, wide, 0.0)
    head = full.astype(BF16)
    lifts[0:64] = head
    lifts[64:128] = head
    lifts[128:192] = (full - head.astype(F32)).astype(BF16)
    lifts[192:256] = jnp.zeros_like(head)


def block_row(block):
    return (
        (block >= 20).astype(jnp.int32)
        + (block >= 40).astype(jnp.int32)
        + (block >= 60).astype(jnp.int32)
        + (block >= 80).astype(jnp.int32)
    )


def pack_rows(cap):
    return TAG_ROWS + cap * FEATURES


def payload_kernel(
    far, dest_band_in, dest_block_in, orders_in, arrival_in, weights_in,
    sums, other_part, kept, pair_out, transit_out, hop_out,
    dest_band, dest_block, orders, arrival, weights, inner_table, angles, packs, tags, line, waves,
    counts, small_sems, in_sems, out_sems,
):
    band = lax.axis_index("band")
    core = lax.rem(band, 2)
    small = [
        pltpu.make_async_copy(source, held, small_sems.at[n])
        for n, (source, held) in enumerate(
            ((orders_in, orders), (dest_band_in, dest_band), (dest_block_in, dest_block))
        )
    ]
    for copy in small:
        copy.start()
    loads = []
    for lat in range(LAT_DEV):
        part = pl.ds(lat * COL_BLOCKS, COL_BLOCKS)
        loads.append(
            (
                pltpu.make_async_copy(arrival_in.at[:, lat], arrival.at[:, lat], in_sems.at[2 * lat]),
                pltpu.make_async_copy(weights_in.at[part], weights.at[part], in_sems.at[2 * lat + 1]),
            )
        )
        for load in loads[-1]:
            load.start()
    far_rows = pack_rows(far)
    for g in range(REACH):
        counts[g] = 0
    tags[...] = jnp.zeros_like(tags)
    sums[...] = jnp.zeros_like(sums)
    for copy in small:
        copy.wait()
    write_tables(orders, core, inner_table, angles)
    lane = iota((TAG_ROWS, BLOCK), 1)

    def weigh(col, lat):
        j = lat * COL_BLOCKS + col
        rows = arrival[:, lat, :, pl.ds(pl.multiple_of(col * BLOCK, BLOCK), BLOCK)]
        payload = jnp.dot(
            rows.reshape(FEATURES, BLOCK), weights[j], preferred_element_type=F32
        ).astype(BF16)
        line[pl.ds(pl.multiple_of(j * FEATURES, FEATURES), FEATURES), :] = payload
        g = dest_band[j] - band + 2
        rank = counts[g]
        counts[g] = rank + 1
        start = pl.multiple_of(g * PACK + TAG_ROWS + rank * FEATURES, 16)
        packs[pl.ds(start, FEATURES), :] = payload
        tag = (dest_block[j] + 1).astype(F32)
        tags[g] = jnp.where(lane == rank, tag, tags[g])
        return lat

    for lat in range(LAT_DEV):
        for load in loads[lat]:
            load.wait()
        lax.fori_loop(0, COL_BLOCKS, weigh, lat, unroll=UNROLL)
    for g in range(REACH):
        packs[g * PACK : g * PACK + TAG_ROWS, :] = tags[g].astype(BF16)

    def ship(group, size, out, at, n):
        source = packs.at[pl.ds(pl.multiple_of(group * PACK, 16), size)]
        return pltpu.make_async_copy(source, out.at[pl.ds(at, size)], out_sems.at[n])

    shipped = [
        ship(4 - 4 * core, far_rows, transit_out, 0, 1),
        ship(1 + 2 * core, far_rows, hop_out, 0, 2),
        ship(4 * core, far_rows, hop_out, far_rows, 3),
        ship(3 - 2 * core, PACK, pair_out, 0, 0),
        ship(2, PACK, kept, 0, 4),
    ]
    for copy in shipped:
        copy.start()

    def transform(n, carry):
        rows = pl.ds(pl.multiple_of(n * 640, 640), 640)
        part = line[rows, :]
        waves[rows, :] = jnp.dot(
            jnp.concatenate([part, part], axis=1), inner_table[...], preferred_element_type=F32
        )
        return carry

    lax.fori_loop(0, 10, transform, 0)

    def analyse(j, carry):
        rows = pl.ds(pl.multiple_of(j * FEATURES, FEATURES), FEATURES)
        block = dest_block[j]
        lat = block_row(block)
        at = (dest_band[j] - band + 2) * LAT_DEV + lat
        col = block - lat * COL_BLOCKS
        cosine = angles[0, pl.ds(col, 1), :]
        sine = angles[1, pl.ds(col, 1), :]
        even = waves[rows, :BLOCK]
        odd = waves[rows, BLOCK:]
        sums[at, :, :BLOCK] = sums[at, :, :BLOCK] + (even * cosine - odd * sine)
        sums[at, :, BLOCK:] = sums[at, :, BLOCK:] - (even * sine + odd * cosine)
        return carry

    lax.fori_loop(0, SLOTS, analyse, 0, unroll=UNROLL)
    longest = jnp.maximum(
        jnp.maximum(counts[4 - 4 * core], counts[1 + 2 * core]), counts[4 * core]
    )
    overflow = jnp.where(longest > far, 1.0, 0.0)
    sums[REACH * LAT_DEV] = jnp.full((FEATURES, 2 * BLOCK), overflow, F32)
    half = iota((FEATURES, BLOCK), 1) < 64

    def split(at, carry):
        real = sums[at, :, :BLOCK]
        imaginary = sums[at, :, BLOCK:]
        other_part[at] = jnp.where(half, pltpu.roll(real, 64, 1), imaginary)
        return carry

    lax.fori_loop(0, REACH * LAT_DEV + 1, split, 0, unroll=13)
    for copy in shipped:
        copy.wait()


def spread_kernel(
    own, other, lifts, hop_own, transit, out, hop_out, turned_rows, work, carried, sems
):
    core = lax.rem(lax.axis_index("band"), 2)
    far_rows = transit.shape[0]
    fetch = pltpu.make_async_copy(transit, carried, sems.at[0])
    store = pltpu.make_async_copy(
        carried, hop_out.at[pl.ds(2 * far_rows, far_rows)], sems.at[1]
    )
    fetch.start()
    for near in range(6):
        for i in range(LAT_DEV):
            if near == 0:
                total = jnp.where(core == 0, own[i], other[i])
            elif near == 5:
                total = jnp.where(core == 1, own[20 + i], other[20 + i])
            else:
                total = own[(near - core) * LAT_DEV + i] + other[(near - 1 + core) * LAT_DEV + i]
            head = total.astype(BF16).astype(F32)
            flipped = jnp.concatenate([head, total - head], axis=0).T.astype(BF16)
            at = ((near // 2) * LAT_DEV + i) * 8 + (near % 2) * 4
            turned_rows[at * 32 : (at + 4) * 32, :] = flipped
    fetch.wait()
    store.start()
    group = (iota((32, 4 * BLOCK), 1) & (BLOCK - 1)) >> 4
    for chunk in range(5):
        part = turned_rows[chunk * 768 : (chunk + 1) * 768, :]
        raised = jnp.dot(
            jnp.concatenate([part, part], axis=1), lifts[...], preferred_element_type=F32
        )
        for r in range(3):
            total = raised[r * 256 : r * 256 + 32]
            for q in range(1, 8):
                low = r * 256 + q * 32
                total = jnp.where(group == q, raised[low : low + 32], total)
            for g in range(GROUPS):
                work[pl.ds(g * 16 + chunk * 3 + r, 32, stride=64), :] = total[
                    :, g * BLOCK : (g + 1) * BLOCK
                ]
    last = REACH * LAT_DEV
    overflow = jnp.maximum(own[last, 0:32, :], other[last, 0:32, :])
    for g in range(GROUPS):
        work[pl.ds(g * 16 + 15, 32, stride=64), :] = overflow
    out[...] = work[...].astype(BF16).reshape(out.shape)
    store.wait()


def legendre_kernel(
    orders_in, parts_in, legendre_in, grid_done, out, overflow,
    orders, parts, work, gathered, legendre, order_sem, part_sem, load_sem,
):
    fetch = pltpu.make_async_copy(orders_in, orders, order_sem)
    fetch.start()
    bring = pltpu.make_async_copy(parts_in, parts, part_sem)
    bring.start()
    load = pltpu.make_async_copy(legendre_in, legendre, load_sem)
    load.start()
    fetch.wait()
    first = ORDERS - orders[lax.axis_index("band")]
    bring.wait()
    work[...] = parts[...].astype(F32).reshape(work.shape)
    flags = work[pl.ds(15, CHIPS * GROUPS, stride=16), :]
    overflow[...] = jnp.broadcast_to(jnp.max(flags, axis=0, keepdims=True), overflow.shape)
    for chip in range(CHIPS):
        for s in range(GROUPS):
            base = (chip * GROUPS + s) * 16
            total = work[base + 5 : base + 10, :]
            if chip > 0:
                total = total + work[base - 64 + 10 : base - 64 + 15, :]
            if chip < CHIPS - 1:
                total = total + work[base + 64 : base + 64 + 5, :]
            at = chip * 40 + s * LAT_DEV
            gathered[at : at + LAT_DEV, :] = total
            gathered[at + 20 : at + 20 + LAT_DEV, :] = pltpu.roll(total, 64, 1)
    right = gathered[...].astype(BF16)
    load.wait()
    step = 256
    for low in range(0, ORDERS + 1, step):
        size = min(step, ORDERS + 1 - low)
        mixed = jnp.dot(legendre[low : low + size, :], right, preferred_element_type=F32).T
        degree = low + iota((16, size), 1)
        for r in range(2):
            picked = jnp.where(
                degree < first, mixed[r * 32 : r * 32 + 16], mixed[r * 32 + 16 : r * 32 + 32]
            )
            out[r, :, low : low + size] = picked


def grid_kernel(far, lift, kept, pair_in, hop_in, passed, *refs):
    out, done, packs, work, tag_rows, tags, found, in_sems, tag_sem, out_sems = refs
    far_rows = pack_rows(far)
    sources = [
        (kept, 0, PACK, CAP),
        (pair_in, 0, PACK, CAP),
        (hop_in, 0, far_rows, far),
        (hop_in, 2 * far_rows, far_rows, far),
        (passed, 0, far_rows, far),
    ]
    starts = [0, PACK, 2 * PACK, 2 * PACK + far_rows, 2 * PACK + 2 * far_rows]
    loads = [
        pltpu.make_async_copy(
            source.at[pl.ds(low, size)], packs.at[pl.ds(starts[n], size)], in_sems.at[n]
        )
        for n, (source, low, size, _) in enumerate(sources)
    ]
    for load in loads:
        load.start()
    for load in loads:
        load.wait()
    for n in range(REACH):
        row = packs[starts[n] : starts[n] + TAG_ROWS, :]
        tag_rows[n : n + 1, :] = row.astype(F32)[0:1].astype(jnp.int32)
    copy = pltpu.make_async_copy(tag_rows, tags, tag_sem)
    copy.start()
    copy.wait()

    def clear(n, carry):
        found[n] = TAG_ROWS
        return carry

    lax.fori_loop(0, SLOTS + 1, clear, 0)
    for n in range(REACH):

        def note(r, carry):
            found[tags[n, r]] = starts[n] + TAG_ROWS + r * FEATURES
            return carry

        lax.fori_loop(0, sources[n][3], note, 0, unroll=10)
    head = lift[...]
    copies = []
    for lat in range(LAT_DEV):
        for col in range(0, COL_BLOCKS, 2):
            tag = lat * COL_BLOCKS + col + 1
            rows = jnp.concatenate(
                [
                    packs[pl.ds(pl.multiple_of(found[tag + n], 16), FEATURES), :]
                    for n in range(2)
                ],
                axis=1,
            )
            value = jnp.dot(
                head, jnp.concatenate([rows, rows], axis=0), preferred_element_type=F32
            )
            work[:, lat, :, col * BLOCK : (col + 2) * BLOCK] = value.reshape(
                FIELDS, LEVELS, 2 * BLOCK
            )
        copies.append(
            pltpu.make_async_copy(work.at[:, lat], out.at[:, lat], out_sems.at[lat])
        )
        copies[-1].start()
    done[...] = jnp.zeros_like(done)
    for copy in copies:
        copy.wait()


def call(kernel, ins, outs, shapes, scratch, name, flops, limit=22, aliases={}):
    return pl.pallas_call(
        kernel,
        in_specs=ins,
        out_specs=outs,
        out_shape=[jax.ShapeDtypeStruct(s, d) for s, d in shapes],
        scratch_shapes=scratch,
        name=name,
        input_output_aliases=aliases,
        cost_estimate=pl.CostEstimate(flops=flops, bytes_accessed=4 * MIB, transcendentals=0),
        compiler_params=pltpu.CompilerParams(vmem_limit_bytes=limit * MIB),
    )


def payloads(far, targets, blocks, order_pairs, arrival, weights):
    part_count = REACH * LAT_DEV + 1
    return call(
        functools.partial(payload_kernel, far),
        [HBM] * 5,
        [VMEM, VMEM] + [HBM] * 4,
        [((part_count, FEATURES, 2 * BLOCK), F32), ((part_count, FEATURES, BLOCK), F32)]
        + [((rows, BLOCK), BF16) for rows in (PACK, PACK, pack_rows(far), 3 * pack_rows(far))],
        [
            pltpu.SMEM((SLOTS,), jnp.int32),
            pltpu.SMEM((SLOTS,), jnp.int32),
            pltpu.SMEM((BANDS,), jnp.int32),
            pltpu.VMEM((FIELDS, LAT_DEV, LEVELS, LONGITUDES), BF16),
            pltpu.VMEM((SLOTS, BLOCK, BLOCK), BF16),
            pltpu.VMEM((2 * BLOCK, 2 * BLOCK), BF16),
            pltpu.VMEM((2, 24, BLOCK), F32),
            pltpu.VMEM((REACH * PACK, BLOCK), BF16),
            pltpu.VMEM((REACH, TAG_ROWS, BLOCK), F32),
            pltpu.VMEM((SLOTS * FEATURES, BLOCK), BF16),
            pltpu.VMEM((SLOTS * FEATURES, 2 * BLOCK), F32),
            pltpu.SMEM((8,), jnp.int32),
            pltpu.SemaphoreType.DMA((3,)),
            pltpu.SemaphoreType.DMA((2 * LAT_DEV,)),
            pltpu.SemaphoreType.DMA((5,)),
        ],
        "payload_and_part_fourier",
        3 * 10**9,
        36,
    )(targets, blocks, order_pairs, arrival, weights)


def grid_solve(far, lift, kept, pair, hop_all, passed):
    return call(
        functools.partial(grid_kernel, far),
        [VMEM] + [ANY] * 4,
        [HBM, VMEM],
        [((FIELDS, LAT_DEV, LEVELS, LONGITUDES), F32), ((8, BLOCK), F32)],
        [
            pltpu.VMEM((2 * PACK + 3 * pack_rows(far), BLOCK), BF16),
            pltpu.VMEM((FIELDS, LAT_DEV, LEVELS, LONGITUDES), F32),
            pltpu.VMEM((8, BLOCK), jnp.int32),
            pltpu.SMEM((8, BLOCK), jnp.int32),
            pltpu.SMEM((SLOTS + 1,), jnp.int32),
            pltpu.SemaphoreType.DMA((REACH,)),
            pltpu.SemaphoreType.DMA,
            pltpu.SemaphoreType.DMA((LAT_DEV,)),
        ],
        "grid_vertical_solve",
        2 * 10**9,
    )(lift, kept, pair, hop_all, passed)


SWAP = [(b, b ^ 1) for b in range(BANDS)]
HOP = [(b, b + 1) for b in range(1, BANDS - 1, 2)] + [(b, b - 1) for b in range(2, BANDS, 2)]


def on_device(
    arrival_adj, block_weights, dest_band, dest_block, lower_coef, upper_coef, order_pairs, legendre
):
    arrival = arrival_adj.transpose(0, 2, 1, 3)
    weights = block_weights.reshape(SLOTS, BLOCK, BLOCK)
    targets = dest_band.reshape(SLOTS)
    blocks = dest_block.reshape(SLOTS)
    sums, other, kept, pair, transit, hop_own = payloads(
        FAR, targets, blocks, order_pairs, arrival, weights
    )
    other = lax.ppermute(other, "band", SWAP)
    transit = lax.ppermute(transit, "band", SWAP)
    lifts, lift, own = call(
        solve_kernel,
        [HBM, HBM, VMEM],
        [VMEM] * 3,
        [
            ((2 * BLOCK, 4 * BLOCK), BF16),
            ((FEATURES, BLOCK), BF16),
            ((REACH * LAT_DEV + 1, FEATURES, BLOCK), F32),
        ],
        [
            pltpu.VMEM((FIELDS, LEVELS), F32),
            pltpu.VMEM((FIELDS, LEVELS), F32),
            pltpu.VMEM((FEATURES, BLOCK), F32),
            pltpu.SemaphoreType.DMA((2,)),
        ],
        "inverse_of_vertical_operator",
        10**9,
    )(lower_coef, upper_coef, sums)
    message, hop_all = call(
        spread_kernel,
        [VMEM] * 3 + [HBM, ANY],
        [VMEM, HBM],
        [((CHIPS * GROUPS, 16, BLOCK), BF16), ((3 * pack_rows(FAR), BLOCK), BF16)],
        [
            pltpu.VMEM((3840, BLOCK), BF16),
            pltpu.VMEM((CHIPS * GROUPS * 16, BLOCK), F32),
            pltpu.VMEM((pack_rows(FAR), BLOCK), BF16),
            pltpu.SemaphoreType.DMA((2,)),
        ],
        "vertical_solve_of_fourier",
        10**9,
        aliases={3: 1},
    )(own, other, lifts, hop_own, transit)
    message, hop_all, pair = lax.optimization_barrier((message, hop_all, pair))
    hop_all = lax.ppermute(hop_all, "band", HOP)
    pair = lax.ppermute(pair, "band", SWAP)
    same_core = [
        [(chip * 2 + core) * GROUPS + s for chip in range(CHIPS) for s in range(GROUPS)]
        for core in range(2)
    ]
    parts = lax.all_to_all(
        message, ("band", "lev"), split_axis=0, concat_axis=0, axis_index_groups=same_core, tiled=True
    )
    passed = lax.ppermute(hop_all[pack_rows(FAR) : 2 * pack_rows(FAR)], "band", SWAP)
    grid_adj, grid_done = grid_solve(FAR, lift, kept, pair, hop_all, passed)
    spectral, overflow = call(
        legendre_kernel,
        [HBM, ANY, HBM, ANY],
        [VMEM] * 2,
        [((2, LEVELS, ORDERS + 1), F32), ((8, BLOCK), F32)],
        [
            pltpu.SMEM((BANDS,), jnp.int32),
            pltpu.VMEM((CHIPS * GROUPS, 16, BLOCK), BF16),
            pltpu.VMEM((CHIPS * GROUPS * 16, BLOCK), F32),
            pltpu.VMEM((LATITUDES, BLOCK), F32),
            pltpu.VMEM((ORDERS + 1, LATITUDES), BF16),
            pltpu.SemaphoreType.DMA,
            pltpu.SemaphoreType.DMA,
            pltpu.SemaphoreType.DMA,
        ],
        "legendre_analysis",
        2 * 10**9,
        56,
    )(order_pairs, parts, legendre[0].T, grid_done)

    def wide_exchange(state):
        _, kept, pair, transit, hop = payloads(
            CAP, targets, blocks, order_pairs, arrival, weights
        )[1:]
        pair = lax.ppermute(pair, "band", SWAP)
        transit = lax.ppermute(transit, "band", SWAP)
        hop = lax.ppermute(jnp.concatenate([hop[: 2 * PACK], transit]), "band", HOP)
        passed = lax.ppermute(hop[PACK : 2 * PACK], "band", SWAP)
        return (jnp.float32(0.0), grid_solve(CAP, lift, kept, pair, hop, passed)[0])

    _, grid_adj = lax.while_loop(
        lambda state: state[0] > 0.0, wide_exchange, (overflow[0, 0], grid_adj)
    )
    return (grid_adj.transpose(0, 2, 1, 3), spectral.transpose(2, 0, 1)[None])


def solution(mesh):
    in_specs = (
        P(None, None, ("band", "lev"), None),
        P("band", "lev", None, None, None),
        P("band", "lev", None),
        P("band", "lev", None),
        P(),
        P(),
        P(),
        P("band", None, None),
    )
    out_specs = (P(None, None, ("band", "lev"), None), P("band", None, None, "lev"))
    return jax.shard_map(
        on_device, mesh=mesh, in_specs=in_specs, out_specs=out_specs, check_vma=False
    )
```

time: 76.5 us -> 59.3 us (0.78)
  the two profiles are of different devices: /device:TPU:25 before, /device:TPU:1 now
where the time goes in v1:
time: 59.3 us; the launch traced here: 59 us
  starting transfers between devices  21.3 us (36%)
  Pallas kernels  20.7 us (35%)
  waiting for transfers between devices  13.5 us (23%)
  local copies, waits for them, and re-layouts  1.84 us (3%)
  between operations  0.9 us (2%)
  loops' own time  0.8 us (1%)
    all_to_all x1, starting transfers between devices, on_device(): lax.all_to_all(message, ('band', 'lev'), split_axis=0, concat_axis=0, axi...  15.2 us
    all_to_all x1, waiting for transfers between devices, on_device(): lax.all_to_all(message, ('band', 'lev'), split_axis=0, concat_axis=0, axi...  9.83 us
    pallas_call x1, Pallas kernels, payloads(): call(functools.partial(payload_kernel, far), [HBM] * 5, [VMEM, VMEM] + [H...  8.53 us
    pallas_call x1, Pallas kernels, grid_solve(): call(functools.partial(grid_kernel, far), [VMEM] + [ANY] * 4, [HBM, VMEM]...  4.42 us
    pallas_call x1, Pallas kernels, on_device(): call(legendre_kernel, [HBM, ANY, HBM, ANY], [VMEM] * 2, [((2, LEVELS, ORD...  3.94 us
    ppermute x1, starting transfers between devices, on_device(): other = lax.ppermute(other, 'band', SWAP)  3.35 us
    pallas_call x1, Pallas kernels, on_device(): call(spread_kernel, [VMEM] * 3 + [HBM, ANY], [VMEM, HBM], [((CHIPS * GROU...  3.15 us
    ppermute x1, starting transfers between devices, on_device(): hop_all = lax.ppermute(hop_all, 'band', HOP)  2.04 us
  transfers between devices with their start and end apart: 6, of which 4 were waited for; matrix products, arithmetic and copies ran while one was open for 0% of the time, Pallas kernels for 9%

profile of v1, /device:TPU:1, one launch (start us, length us, event | category | flops | bytes accessed | tf_op | source)
XLA Modules:
  0.0 59.0 jit_solution(5045336391934753909)
XLA Ops:
  0.6 0.0 copy-start
  0.6 0.0 copy-start.1
  0.6 8.5 %payload_and_part_fourier.3 = (f32[26,64,256]{2,1,0:T(8,128)S(1)}, f32[26,64,128]{2,1,0:T(8,128)S(1)}, bf16[2576,128]{1,0:T(8,128)(2,1)S(1)}, bf16[2576,128]{1,0...) custom-call(s32[100]{0:T(128)} %bitcast.15, s32[100]{0:T(128)} %bitcast.17, ...), custom_call_target="tpu_custom_call" | custom-call | flops 3000000000 | bytes 4194304 | tf_op jit(solution)/shard_map/payload_and_part_fourier/pallas_call | solution.py:440
  9.2 3.3 %collective-permute-start.4 = (f32[26,64,128]{2,1,0:T(8,128)S(1)}, f32[26,64,128]{2,1,0:T(8,128)S(1)}, u32[]{:S(2)}, u32[]{:S(2)}) collective-permute-start(f32[26,64,128]{2,1,0:T(8,128)S(1)} %get-tuple-element.67), channel_id=1, source_target_pairs={{0,4},{4,0},{8,12},{12,8},{16,20},{20,16},{24,28},{28,24},{32,36},... | collective-permute-start | bytes 2555912 | tf_op jit(solution)/shard_map/ppermute | solution.py:504
  12.5 0.1 collective-permute-start.5
  12.6 0.0 copy-done.1
  12.6 0.7 %inverse_of_vertical_operator.1 = (bf16[256,512]{1,0:T(8,128)(2,1)S(1)}, bf16[64,128]{1,0:T(8,128)(2,1)S(1)}, f32[26,64,128]{2,1,0:T(8,128)S(1)}) custom-call(f32[4,16]{1,0:T(4,128)S(1)} %copy-done, f32[4,16]{1,0:T(4,128)S(1)} %copy-done.1, f32[26,64,256]{2,1,0:T(8,128)S(1)} %get-tuple-element.65.sums), custom_call_target="tpu_custom_call" | custom-call | flops 1000000000 | bytes 4194304 | tf_op jit(solution)/shard_map/inverse_of_vertical_operator/pallas_call | solution.py:506
  13.3 1.7 %collective-permute-done.5.transit = bf16[1296,128]{1,0:T(8,128)(2,1)S(1)} collective-permute-done((bf16[1296,128]{1,0:T(8,128)(2,1)S(1)}, bf16[1296,128]{1,0:T(8,128)(2,1)S(1)}, u32[]{:S(2)}, u32[]{:S(2)}) %collective-permute-start.5) | collective-permute-done | bytes 331808 | tf_op jit(solution)/shard_map/ppermute | solution.py:505
  15.0 0.0 collective-permute-done.4.other
  15.0 3.2 %vertical_solve_of_fourier.1 = (bf16[128,16,128]{2,1,0:T(8,128)(2,1)}, bf16[3888,128]{1,0:T(8,128)(2,1)S(1)}) custom-call(f32[26,64,128]{2,1,0:T(8,128)S(1)} %get-tuple-element.66.own, f32[26,64,128]{2,1,0:T(8,128)S(1)} %collective-permute-done.4.other, bf16[256,512]{1,0:T(8,128)(2,1)S(1)} %get-tuple-element.68.lifts, ...), custom_call_target="tpu_custom_call", output_to_operand_aliasing={{1}: (3, {})} | custom-call | flops 1000000000 | bytes 4194304 | tf_op jit(solution)/shard_map/vertical_solve_of_fourier/pallas_call | solution.py:524
  18.2 2.0 %collective-permute-start.7 = (bf16[3888,128]{1,0:T(8,128)(2,1)S(1)}, bf16[3888,128]{1,0:T(8,128)(2,1)S(1)}, u32[]{:S(2)}, u32[]{:S(2)}) collective-permute-start(bf16[3888,128]{1,0:T(8,128)(2,1)S(1)} %get-tuple-element.78), channel_id=1, source_target_pairs={{4,8},{12,16},{20,24},{28,32},{36,40},{44,48},{52,56},{60,64},{68,... | collective-permute-start | bytes 2985992 | tf_op jit(solution)/shard_map/ppermute | solution.py:540
  20.2 15.2 %all-to-all-start = ((bf16[128,16,128]{2,1,0:T(8,128)(2,1)}), bf16[128,16,128]{2,1,0:T(8,128)(2,1)}, u32[]{:S(2)}, u32[]{:S(2)}) async-start(bf16[128,16,128]{2,1,0:T(8,128)(2,1)} %get-tuple-element.74), calls=%async_computation | async-start | bytes 1048576 | tf_op jit(solution)/shard_map/all_to_all | solution.py:546
  35.4 0.1 collective-permute-start.6
  35.5 0.0 collective-permute-done.7.hop_in
  35.5 0.6 collective-permute-start.8
  36.1 1.5 %collective-permute-done.6.pair_in = bf16[2576,128]{1,0:T(8,128)(2,1)S(1)} collective-permute-done((bf16[2576,128]{1,0:T(8,128)(2,1)S(1)}, bf16[2576,128]{1,0:T(8,128)(2,1)S(1)}, u32[]{:S(2)}, u32[]{:S(2)}) %collective-permute-start.6) | collective-permute-done | bytes 659488 | tf_op jit(solution)/shard_map/ppermute | solution.py:541
  37.6 0.5 collective-permute-done.8.passed
  38.1 4.4 %grid_vertical_solve.3 = (f32[4,5,16,2560]{3,2,1,0:T(8,128)}, f32[8,128]{1,0:T(8,128)S(1)}) custom-call(bf16[64,128]{1,0:T(8,128)(2,1)S(1)} %get-tuple-element.115.lift, bf16[2576,128]{1,0:T(8,128)(2,1)S(1)} %get-tuple-element.76.kept, bf16[2576,128]{1,0:T(8,128)(2,1)S(1)} %collective-permute-done.6.pair_in, ...), custom_call_target="tpu_custom_call" | custom-call | flops 2000000000 | bytes 4194304 | tf_op jit(solution)/shard_map/grid_vertical_solve/pallas_call | solution.py:470
  42.5 0.6 copy-done.4
  43.1 9.8 %all-to-all-done.parts_in = bf16[128,16,128]{2,1,0:T(8,128)(2,1)} async-done(((bf16[128,16,128]{2,1,0:T(8,128)(2,1)}), bf16[128,16,128]{2,1,0:T(8,128)(2,1)}, u32[]{:S(2)}, u32[]{:S(2)}) %all-to-all-start) | async-done | bytes 524320 | tf_op jit(solution)/shard_map/all_to_all | solution.py:546
  52.9 0.0 copy-done.5
  52.9 3.9 %legendre_analysis.1 = (f32[2,16,1281]{2,1,0:T(8,128)}, f32[8,128]{1,0:T(8,128)}) custom-call(s32[64]{0:T(128)S(1)} %copy-done.5, bf16[128,16,128]{2,1,0:T(8,128)(2,1)} %all-to-all-done.parts_in, bf16[1281,1280]{1,0:T(8,128)(2,1)} %bitcast.12, f32[8,128]{1,0:T(8,128)} %copy-done.4), custom_call_target="tpu_custom_call" | custom-call | flops 2000000000 | bytes 4194304 | tf_op jit(solution)/shard_map/legendre_analysis/pallas_call | solution.py:551
  56.9 1.2 %slice.13 = f32[1,1]{1,0:T(1,128)} slice(f32[8,128]{1,0:T(8,128)} %get-tuple-element.80), slice={[0:1], [0:1]} | slice | bytes 8 | tf_op jit(solution)/shard_map/slice | solution.py:582
  58.1 0.8 %while.9 = (f32[]{:T(128)}, f32[4,5,16,2560]{3,2,1,0:T(8,128)}, s32[100]{0:T(128)S(1)}, s32[100]{0:T(128)S(1)}, s32[64]{0:T(128)S(1)}, /*index=5*/bf16[4,5,16,25...) while((f32[]{:T(128)}, f32[4,5,16,2560]{3,2,1,0:T(8,128)}, s32[100]{0:T(128)S(1)}, ...), condition=%region_1.0_spmd, body=%region_0.0_spmd | while | flops 5003956736 | bytes 37404968 | solution.py:581
  (8 shorter events, 0.0 us)
Async XLA Ops:
  0.6 12.0 %copy-start = (f32[4,16]{1,0:T(4,128)S(1)}, f32[4,16]{1,0:T(4,128)}, u32[]{:S(2)}) copy-start(f32[4,16]{1,0:T(4,128)} %lower_in.1) | copy-start | bytes 772
  0.6 12.0 %copy-start.1 = (f32[4,16]{1,0:T(4,128)S(1)}, f32[4,16]{1,0:T(4,128)}, u32[]{:S(2)}) copy-start(f32[4,16]{1,0:T(4,128)} %upper_in.1) | copy-start | bytes 772
  9.2 5.8 %collective-permute-start.4 = (f32[26,64,128]{2,1,0:T(8,128)S(1)}, f32[26,64,128]{2,1,0:T(8,128)S(1)}, u32[]{:S(2)}, u32[]{:S(2)}) collective-permute-start(f32[26,64,128]{2,1,0:T(8,128)S(1)} %get-tuple-element.67), channel_id=1, source_target_pairs={{0,4},{4,0},{8,12},{12,8},{16,20},{20,16},{24,28},{28,24},{32,36},... | collective-permute-start | bytes 2555912 | tf_op jit(solution)/shard_map/ppermute | solution.py:504
  12.5 2.5 %collective-permute-start.5 = (bf16[1296,128]{1,0:T(8,128)(2,1)S(1)}, bf16[1296,128]{1,0:T(8,128)(2,1)S(1)}, u32[]{:S(2)}, u32[]{:S(2)}) collective-permute-start(bf16[1296,128]{1,0:T(8,128)(2,1)S(1)} %get-tuple-element.70), channel_id=1, source_target_pairs={{0,4},{4,0},{8,12},{12,8},{16,20},{20,16},{24,28},{28,24},{32,36},... | collective-permute-start | bytes 995336 | tf_op jit(solution)/shard_map/ppermute | solution.py:505
  18.2 17.3 %collective-permute-start.7 = (bf16[3888,128]{1,0:T(8,128)(2,1)S(1)}, bf16[3888,128]{1,0:T(8,128)(2,1)S(1)}, u32[]{:S(2)}, u32[]{:S(2)}) collective-permute-start(bf16[3888,128]{1,0:T(8,128)(2,1)S(1)} %get-tuple-element.78), channel_id=1, source_target_pairs={{4,8},{12,16},{20,24},{28,32},{36,40},{44,48},{52,56},{60,64},{68,... | collective-permute-start | bytes 2985992 | tf_op jit(solution)/shard_map/ppermute | solution.py:540
  20.2 32.7 %all-to-all-start = ((bf16[128,16,128]{2,1,0:T(8,128)(2,1)}), bf16[128,16,128]{2,1,0:T(8,128)(2,1)}, u32[]{:S(2)}, u32[]{:S(2)}) async-start(bf16[128,16,128]{2,1,0:T(8,128)(2,1)} %get-tuple-element.74), calls=%async_computation | async-start | bytes 1048576 | tf_op jit(solution)/shard_map/all_to_all | solution.py:546
  35.4 2.2 %collective-permute-start.6 = (bf16[2576,128]{1,0:T(8,128)(2,1)S(1)}, bf16[2576,128]{1,0:T(8,128)(2,1)S(1)}, u32[]{:S(2)}, u32[]{:S(2)}) collective-permute-start(bf16[2576,128]{1,0:T(8,128)(2,1)S(1)} %get-tuple-element.77), channel_id=1, source_target_pairs={{0,4},{4,0},{8,12},{12,8},{16,20},{20,16},{24,28},{28,24},{32,36},... | collective-permute-start | bytes 1978376 | tf_op jit(solution)/shard_map/ppermute | solution.py:541
  35.5 2.5 %collective-permute-start.8 = (bf16[1296,128]{1,0:T(8,128)(2,1)S(1)}, bf16[1296,128]{1,0:T(8,128)(2,1)S(1)}, u32[]{:S(2)}, u32[]{:S(2)}) collective-permute-start(bf16[1296,128]{1,0:T(8,128)(2,1)S(1)} %slice.15), channel_id=1, source_target_pairs={{0,4},{4,0},{8,12},{12,8},{16,20},{20,16},{24,28},{28,24},{32,36},... | collective-permute-start | bytes 995336 | tf_op jit(solution)/shard_map/ppermute | solution.py:549
  38.1 14.9 %copy-start.5 = (s32[64]{0:T(128)S(1)}, s32[64]{0:T(128)}, u32[]{:S(2)}) copy-start(s32[64]{0:T(128)} %orders_in.3) | copy-start | bytes 772
  42.5 0.6 %copy-start.4 = (f32[8,128]{1,0:T(8,128)}, f32[8,128]{1,0:T(8,128)S(1)}, u32[]{:S(2)}) copy-start(f32[8,128]{1,0:T(8,128)S(1)} %get-tuple-element.79.grid_done) | copy-start | bytes 12292
  52.9 5.2 %copy-start.6 = (s32[1,1,100]{2,1,0:T(1,128)S(1)}, s32[1,1,100]{2,1,0:T(1,128)}, u32[]{:S(2)}) copy-start(s32[1,1,100]{2,1,0:T(1,128)} %param.12) | copy-start | bytes 1204
  52.9 5.2 %copy-start.7 = (s32[1,1,100]{2,1,0:T(1,128)S(1)}, s32[1,1,100]{2,1,0:T(1,128)}, u32[]{:S(2)}) copy-start(s32[1,1,100]{2,1,0:T(1,128)} %param.13) | copy-start | bytes 1204

commit v2 on v1

--- a/solution.py
+++ b/solution.py
@@ -23,7 +23,8 @@
 BLOCK = 128
 TAG_ROWS = 16
 PACK = TAG_ROWS + CAP * FEATURES
-UNROLL = 10
+UNROLL = 20
+AHEAD = 2
 SLOTS = 100
 COL_BLOCKS = 20
 LATITUDES = 1280
@@ -174,7 +175,8 @@
                 pltpu.make_async_copy(weights_in.at[part], weights.at[part], in_sems.at[2 * lat + 1]),
             )
         )
-        for load in loads[-1]:
+    for ahead in range(AHEAD):
+        for load in loads[ahead]:
             load.start()
     far_rows = pack_rows(far)
     for g in range(REACH):
@@ -192,7 +194,9 @@
         payload = jnp.dot(
             rows.reshape(FEATURES, BLOCK), weights[j], preferred_element_type=F32
         ).astype(BF16)
-        line[pl.ds(pl.multiple_of(j * FEATURES, FEATURES), FEATURES), :] = payload
+        line[pl.ds(pl.multiple_of(j * FEATURES, FEATURES), FEATURES), :] = jnp.concatenate(
+            [payload, payload], axis=1
+        )
         g = dest_band[j] - band + 2
         rank = counts[g]
         counts[g] = rank + 1
@@ -202,13 +206,6 @@
         tags[g] = jnp.where(lane == rank, tag, tags[g])
         return lat
 
-    for lat in range(LAT_DEV):
-        for load in loads[lat]:
-            load.wait()
-        lax.fori_loop(0, COL_BLOCKS, weigh, lat, unroll=UNROLL)
-    for g in range(REACH):
-        packs[g * PACK : g * PACK + TAG_ROWS, :] = tags[g].astype(BF16)
-
     def ship(group, size, out, at, n):
         source = packs.at[pl.ds(pl.multiple_of(group * PACK, 16), size)]
         return pltpu.make_async_copy(source, out.at[pl.ds(at, size)], out_sems.at[n])
@@ -220,18 +217,10 @@
         ship(3 - 2 * core, PACK, pair_out, 0, 0),
         ship(2, PACK, kept, 0, 4),
     ]
-    for copy in shipped:
-        copy.start()
-
-    def transform(n, carry):
-        rows = pl.ds(pl.multiple_of(n * 640, 640), 640)
-        part = line[rows, :]
-        waves[rows, :] = jnp.dot(
-            jnp.concatenate([part, part], axis=1), inner_table[...], preferred_element_type=F32
-        )
-        return carry
-
-    lax.fori_loop(0, 10, transform, 0)
+
+    def transform(lat):
+        rows = pl.ds(lat * COL_BLOCKS * FEATURES, COL_BLOCKS * FEATURES)
+        waves[rows, :] = jnp.dot(line[rows, :], inner_table[...], preferred_element_type=F32)
 
     def analyse(j, carry):
         rows = pl.ds(pl.multiple_of(j * FEATURES, FEATURES), FEATURES)
@@ -247,7 +236,20 @@
         sums[at, :, BLOCK:] = sums[at, :, BLOCK:] - (even * sine + odd * cosine)
         return carry
 
-    lax.fori_loop(0, SLOTS, analyse, 0, unroll=UNROLL)
+    for lat in range(LAT_DEV):
+        for load in loads[lat]:
+            load.wait()
+        if lat + AHEAD < LAT_DEV:
+            for load in loads[lat + AHEAD]:
+                load.start()
+        lax.fori_loop(0, COL_BLOCKS, weigh, lat, unroll=UNROLL)
+        if lat == LAT_DEV - 1:
+            for g in range(REACH):
+                packs[g * PACK : g * PACK + TAG_ROWS, :] = tags[g].astype(BF16)
+            for copy in shipped:
+                copy.start()
+        transform(lat)
+        lax.fori_loop(COL_BLOCKS * lat, COL_BLOCKS * (lat + 1), analyse, 0, unroll=UNROLL)
     longest = jnp.maximum(
         jnp.maximum(counts[4 - 4 * core], counts[1 + 2 * core]), counts[4 * core]
     )
@@ -328,7 +330,7 @@
     bring.wait()
     work[...] = parts[...].astype(F32).reshape(work.shape)
     flags = work[pl.ds(15, CHIPS * GROUPS, stride=16), :]
-    overflow[...] = jnp.broadcast_to(jnp.max(flags, axis=0, keepdims=True), overflow.shape)
+    overflow[0, 0] = jnp.max(flags)
     for chip in range(CHIPS):
         for s in range(GROUPS):
             base = (chip * GROUPS + s) * 16
@@ -453,7 +455,7 @@
             pltpu.VMEM((2, 24, BLOCK), F32),
             pltpu.VMEM((REACH * PACK, BLOCK), BF16),
             pltpu.VMEM((REACH, TAG_ROWS, BLOCK), F32),
-            pltpu.VMEM((SLOTS * FEATURES, BLOCK), BF16),
+            pltpu.VMEM((SLOTS * FEATURES, 2 * BLOCK), BF16),
             pltpu.VMEM((SLOTS * FEATURES, 2 * BLOCK), F32),
             pltpu.SMEM((8,), jnp.int32),
             pltpu.SemaphoreType.DMA((3,)),
@@ -551,8 +553,8 @@
     spectral, overflow = call(
         legendre_kernel,
         [HBM, ANY, HBM, ANY],
-        [VMEM] * 2,
-        [((2, LEVELS, ORDERS + 1), F32), ((8, BLOCK), F32)],
+        [VMEM, SMEM],
+        [((2, LEVELS, ORDERS + 1), F32), ((1, 1), F32)],
         [
             pltpu.SMEM((BANDS,), jnp.int32),
             pltpu.VMEM((CHIPS * GROUPS, 16, BLOCK), BF16),

time: 59.3 us -> 55.6 us (0.938)
  Pallas kernels: 20.7 us -> 18.4 us
  local copies, waits for them, and re-layouts: 1.84 us -> 0.63 us
    pallas_call x1, Pallas kernels: 8.53 us -> 6.18 us  [payloads(): call(functools.partial(payload_kernel, far), [HBM] * 5, [VMEM, VMEM] + [H...]
    slice x1 -> x0, local copies, waits for them, and re-layouts: 1.22 us -> none  [on_device(): overflow[0, 0]]
where the time goes in v2:
time: 55.6 us; the launch traced here: 55.3 us
  starting transfers between devices  21.5 us (39%)
  Pallas kernels  18.4 us (33%)
  waiting for transfers between devices  13.3 us (24%)
  between operations  0.92 us (2%)
  local copies, waits for them, and re-layouts  0.63 us (1%)
  loops' own time  0.62 us (1%)
    all_to_all x1, starting transfers between devices, on_device(): lax.all_to_all(message, ('band', 'lev'), split_axis=0, concat_axis=0, axi...  15.1 us
    all_to_all x1, waiting for transfers between devices, on_device(): lax.all_to_all(message, ('band', 'lev'), split_axis=0, concat_axis=0, axi...  9.82 us
    pallas_call x1, Pallas kernels, payloads(): call(functools.partial(payload_kernel, far), [HBM] * 5, [VMEM, VMEM] + [H...  6.18 us
    pallas_call x1, Pallas kernels, grid_solve(): call(functools.partial(grid_kernel, far), [VMEM] + [ANY] * 4, [HBM, VMEM]...  4.42 us
    pallas_call x1, Pallas kernels, on_device(): call(legendre_kernel, [HBM, ANY, HBM, ANY], [VMEM, SMEM], [((2, LEVELS, O...  3.95 us
    ppermute x1, starting transfers between devices, on_device(): other = lax.ppermute(other, 'band', SWAP)  3.33 us
    pallas_call x1, Pallas kernels, on_device(): call(spread_kernel, [VMEM] * 3 + [HBM, ANY], [VMEM, HBM], [((CHIPS * GROU...  3.15 us
    ppermute x1, starting transfers between devices, on_device(): hop_all = lax.ppermute(hop_all, 'band', HOP)  2.07 us
  transfers between devices with their start and end apart: 6, of which 4 were waited for; matrix products, arithmetic and copies ran while one was open for 0% of the time, Pallas kernels for 9%

profile of v2, /device:TPU:1, one launch (start us, length us, event | category | flops | bytes accessed | tf_op | source)
XLA Modules:
  0.0 55.3 jit_solution(2147036292758525444)
XLA Ops:
  0.6 0.0 copy-start
  0.6 0.0 copy-start.1
  0.6 6.2 %payload_and_part_fourier.3 = (f32[26,64,256]{2,1,0:T(8,128)S(1)}, f32[26,64,128]{2,1,0:T(8,128)S(1)}, bf16[2576,128]{1,0:T(8,128)(2,1)S(1)}, bf16[2576,128]{1,0...) custom-call(s32[100]{0:T(128)} %bitcast.15, s32[100]{0:T(128)} %bitcast.17, ...), custom_call_target="tpu_custom_call" | custom-call | flops 3000000000 | bytes 4194304 | tf_op jit(solution)/shard_map/payload_and_part_fourier/pallas_call | solution.py:442
  6.8 3.3 %collective-permute-start.4 = (f32[26,64,128]{2,1,0:T(8,128)S(1)}, f32[26,64,128]{2,1,0:T(8,128)S(1)}, u32[]{:S(2)}, u32[]{:S(2)}) collective-permute-start(f32[26,64,128]{2,1,0:T(8,128)S(1)} %get-tuple-element.67), channel_id=1, source_target_pairs={{0,4},{4,0},{8,12},{12,8},{16,20},{20,16},{24,28},{28,24},{32,36},... | collective-permute-start | bytes 2555912 | tf_op jit(solution)/shard_map/ppermute | solution.py:506
  10.2 0.1 collective-permute-start.5
  10.3 0.0 copy-done
  10.3 0.0 copy-done.1
  10.3 0.7 %inverse_of_vertical_operator.1 = (bf16[256,512]{1,0:T(8,128)(2,1)S(1)}, bf16[64,128]{1,0:T(8,128)(2,1)S(1)}, f32[26,64,128]{2,1,0:T(8,128)S(1)}) custom-call(f32[4,16]{1,0:T(4,128)S(1)} %copy-done, f32[4,16]{1,0:T(4,128)S(1)} %copy-done.1, f32[26,64,256]{2,1,0:T(8,128)S(1)} %get-tuple-element.65.sums), custom_call_target="tpu_custom_call" | custom-call | flops 1000000000 | bytes 4194304 | tf_op jit(solution)/shard_map/inverse_of_vertical_operator/pallas_call | solution.py:508
  10.9 1.7 %collective-permute-done.5.transit = bf16[1296,128]{1,0:T(8,128)(2,1)S(1)} collective-permute-done((bf16[1296,128]{1,0:T(8,128)(2,1)S(1)}, bf16[1296,128]{1,0:T(8,128)(2,1)S(1)}, u32[]{:S(2)}, u32[]{:S(2)}) %collective-permute-start.5) | collective-permute-done | bytes 331808 | tf_op jit(solution)/shard_map/ppermute | solution.py:507
  12.7 0.0 collective-permute-done.4.other
  12.7 3.1 %vertical_solve_of_fourier.1 = (bf16[128,16,128]{2,1,0:T(8,128)(2,1)}, bf16[3888,128]{1,0:T(8,128)(2,1)S(1)}) custom-call(f32[26,64,128]{2,1,0:T(8,128)S(1)} %get-tuple-element.66.own, f32[26,64,128]{2,1,0:T(8,128)S(1)} %collective-permute-done.4.other, bf16[256,512]{1,0:T(8,128)(2,1)S(1)} %get-tuple-element.68.lifts, ...), custom_call_target="tpu_custom_call", output_to_operand_aliasing={{1}: (3, {})} | custom-call | flops 1000000000 | bytes 4194304 | tf_op jit(solution)/shard_map/vertical_solve_of_fourier/pallas_call | solution.py:526
  15.8 2.1 %collective-permute-start.7 = (bf16[3888,128]{1,0:T(8,128)(2,1)S(1)}, bf16[3888,128]{1,0:T(8,128)(2,1)S(1)}, u32[]{:S(2)}, u32[]{:S(2)}) collective-permute-start(bf16[3888,128]{1,0:T(8,128)(2,1)S(1)} %get-tuple-element.78), channel_id=1, source_target_pairs={{4,8},{12,16},{20,24},{28,32},{36,40},{44,48},{52,56},{60,64},{68,... | collective-permute-start | bytes 2985992 | tf_op jit(solution)/shard_map/ppermute | solution.py:542
  17.9 15.1 %all-to-all-start = ((bf16[128,16,128]{2,1,0:T(8,128)(2,1)}), bf16[128,16,128]{2,1,0:T(8,128)(2,1)}, u32[]{:S(2)}, u32[]{:S(2)}) async-start(bf16[128,16,128]{2,1,0:T(8,128)(2,1)} %get-tuple-element.74), calls=%async_computation | async-start | bytes 1048576 | tf_op jit(solution)/shard_map/all_to_all | solution.py:548
  33.0 0.1 collective-permute-start.6
  33.1 0.0 collective-permute-done.7.hop_in
  33.2 0.8 %collective-permute-start.8 = (bf16[1296,128]{1,0:T(8,128)(2,1)S(1)}, bf16[1296,128]{1,0:T(8,128)(2,1)S(1)}, u32[]{:S(2)}, u32[]{:S(2)}) collective-permute-start(bf16[1296,128]{1,0:T(8,128)(2,1)S(1)} %slice.11), channel_id=1, source_target_pairs={{0,4},{4,0},{8,12},{12,8},{16,20},{20,16},{24,28},{28,24},{32,36},... | collective-permute-start | bytes 995336 | tf_op jit(solution)/shard_map/ppermute | solution.py:551
  33.9 1.3 %collective-permute-done.6.pair_in = bf16[2576,128]{1,0:T(8,128)(2,1)S(1)} collective-permute-done((bf16[2576,128]{1,0:T(8,128)(2,1)S(1)}, bf16[2576,128]{1,0:T(8,128)(2,1)S(1)}, u32[]{:S(2)}, u32[]{:S(2)}) %collective-permute-start.6) | collective-permute-done | bytes 659488 | tf_op jit(solution)/shard_map/ppermute | solution.py:543
  35.2 0.5 collective-permute-done.8.passed
  35.7 4.4 %grid_vertical_solve.3 = (f32[4,5,16,2560]{3,2,1,0:T(8,128)}, f32[8,128]{1,0:T(8,128)S(1)}) custom-call(bf16[64,128]{1,0:T(8,128)(2,1)S(1)} %get-tuple-element.115.lift, bf16[2576,128]{1,0:T(8,128)(2,1)S(1)} %get-tuple-element.76.kept, bf16[2576,128]{1,0:T(8,128)(2,1)S(1)} %collective-permute-done.6.pair_in, ...), custom_call_target="tpu_custom_call" | custom-call | flops 2000000000 | bytes 4194304 | tf_op jit(solution)/shard_map/grid_vertical_solve/pallas_call | solution.py:472
  40.1 0.0 copy-start.4
  40.1 0.6 %copy-done.4 = f32[8,128]{1,0:T(8,128)} copy-done((f32[8,128]{1,0:T(8,128)}, f32[8,128]{1,0:T(8,128)S(1)}, u32[]{:S(2)}) %copy-start.4) | copy-done | bytes 4120
  40.7 9.8 %all-to-all-done.parts_in = bf16[128,16,128]{2,1,0:T(8,128)(2,1)} async-done(((bf16[128,16,128]{2,1,0:T(8,128)(2,1)}), bf16[128,16,128]{2,1,0:T(8,128)(2,1)}, u32[]{:S(2)}, u32[]{:S(2)}) %all-to-all-start) | async-done | bytes 524320 | tf_op jit(solution)/shard_map/all_to_all | solution.py:548
  50.6 4.0 %legendre_analysis.1 = (f32[2,16,1281]{2,1,0:T(8,128)}, f32[1,1]{1,0:T(1,128)}) custom-call(s32[64]{0:T(128)S(1)} %copy-done.5, bf16[128,16,128]{2,1,0:T(8,128)(2,1)} %all-to-all-done.parts_in, bf16[1281,1280]{1,0:T(8,128)(2,1)} %bitcast.12, f32[8,128]{1,0:T(8,128)} %copy-done.4), custom_call_target="tpu_custom_call" | custom-call | flops 2000000000 | bytes 4194304 | tf_op jit(solution)/shard_map/legendre_analysis/pallas_call | solution.py:553
  54.5 0.6 %while.9 = (f32[]{:T(128)}, f32[4,5,16,2560]{3,2,1,0:T(8,128)}, s32[100]{0:T(128)S(1)}, s32[100]{0:T(128)S(1)}, s32[64]{0:T(128)S(1)}, /*index=5*/bf16[4,5,16,25...) while((f32[]{:T(128)}, f32[4,5,16,2560]{3,2,1,0:T(8,128)}, s32[100]{0:T(128)S(1)}, ...), condition=%region_1.0_spmd, body=%region_0.0_spmd | while | flops 5003956736 | bytes 37404968 | solution.py:583
  (7 shorter events, 0.0 us)
Async XLA Ops:
  0.6 9.6 %copy-start = (f32[4,16]{1,0:T(4,128)S(1)}, f32[4,16]{1,0:T(4,128)}, u32[]{:S(2)}) copy-start(f32[4,16]{1,0:T(4,128)} %lower_in.1) | copy-start | bytes 772
  0.6 9.6 %copy-start.1 = (f32[4,16]{1,0:T(4,128)S(1)}, f32[4,16]{1,0:T(4,128)}, u32[]{:S(2)}) copy-start(f32[4,16]{1,0:T(4,128)} %upper_in.1) | copy-start | bytes 772
  6.8 5.8 %collective-permute-start.4 = (f32[26,64,128]{2,1,0:T(8,128)S(1)}, f32[26,64,128]{2,1,0:T(8,128)S(1)}, u32[]{:S(2)}, u32[]{:S(2)}) collective-permute-start(f32[26,64,128]{2,1,0:T(8,128)S(1)} %get-tuple-element.67), channel_id=1, source_target_pairs={{0,4},{4,0},{8,12},{12,8},{16,20},{20,16},{24,28},{28,24},{32,36},... | collective-permute-start | bytes 2555912 | tf_op jit(solution)/shard_map/ppermute | solution.py:506
  10.2 2.5 %collective-permute-start.5 = (bf16[1296,128]{1,0:T(8,128)(2,1)S(1)}, bf16[1296,128]{1,0:T(8,128)(2,1)S(1)}, u32[]{:S(2)}, u32[]{:S(2)}) collective-permute-start(bf16[1296,128]{1,0:T(8,128)(2,1)S(1)} %get-tuple-element.70), channel_id=1, source_target_pairs={{0,4},{4,0},{8,12},{12,8},{16,20},{20,16},{24,28},{28,24},{32,36},... | collective-permute-start | bytes 995336 | tf_op jit(solution)/shard_map/ppermute | solution.py:507
  15.8 17.3 %collective-permute-start.7 = (bf16[3888,128]{1,0:T(8,128)(2,1)S(1)}, bf16[3888,128]{1,0:T(8,128)(2,1)S(1)}, u32[]{:S(2)}, u32[]{:S(2)}) collective-permute-start(bf16[3888,128]{1,0:T(8,128)(2,1)S(1)} %get-tuple-element.78), channel_id=1, source_target_pairs={{4,8},{12,16},{20,24},{28,32},{36,40},{44,48},{52,56},{60,64},{68,... | collective-permute-start | bytes 2985992 | tf_op jit(solution)/shard_map/ppermute | solution.py:542
  17.9 32.7 %all-to-all-start = ((bf16[128,16,128]{2,1,0:T(8,128)(2,1)}), bf16[128,16,128]{2,1,0:T(8,128)(2,1)}, u32[]{:S(2)}, u32[]{:S(2)}) async-start(bf16[128,16,128]{2,1,0:T(8,128)(2,1)} %get-tuple-element.74), calls=%async_computation | async-start | bytes 1048576 | tf_op jit(solution)/shard_map/all_to_all | solution.py:548
  33.0 2.2 %collective-permute-start.6 = (bf16[2576,128]{1,0:T(8,128)(2,1)S(1)}, bf16[2576,128]{1,0:T(8,128)(2,1)S(1)}, u32[]{:S(2)}, u32[]{:S(2)}) collective-permute-start(bf16[2576,128]{1,0:T(8,128)(2,1)S(1)} %get-tuple-element.77), channel_id=1, source_target_pairs={{0,4},{4,0},{8,12},{12,8},{16,20},{20,16},{24,28},{28,24},{32,36},... | collective-permute-start | bytes 1978376 | tf_op jit(solution)/shard_map/ppermute | solution.py:543
  33.2 2.5 %collective-permute-start.8 = (bf16[1296,128]{1,0:T(8,128)(2,1)S(1)}, bf16[1296,128]{1,0:T(8,128)(2,1)S(1)}, u32[]{:S(2)}, u32[]{:S(2)}) collective-permute-start(bf16[1296,128]{1,0:T(8,128)(2,1)S(1)} %slice.11), channel_id=1, source_target_pairs={{0,4},{4,0},{8,12},{12,8},{16,20},{20,16},{24,28},{28,24},{32,36},... | collective-permute-start | bytes 995336 | tf_op jit(solution)/shard_map/ppermute | solution.py:551
  35.7 14.8 %copy-start.5 = (s32[64]{0:T(128)S(1)}, s32[64]{0:T(128)}, u32[]{:S(2)}) copy-start(s32[64]{0:T(128)} %orders_in.3) | copy-start | bytes 772
  40.1 0.6 %copy-start.4 = (f32[8,128]{1,0:T(8,128)}, f32[8,128]{1,0:T(8,128)S(1)}, u32[]{:S(2)}) copy-start(f32[8,128]{1,0:T(8,128)S(1)} %get-tuple-element.79.grid_done) | copy-start | bytes 12292
  50.6 4.0 %copy-start.6 = (s32[1,1,100]{2,1,0:T(1,128)S(1)}, s32[1,1,100]{2,1,0:T(1,128)}, u32[]{:S(2)}) copy-start(s32[1,1,100]{2,1,0:T(1,128)} %param.12) | copy-start | bytes 1204
  50.6 4.0 %copy-start.7 = (s32[1,1,100]{2,1,0:T(1,128)S(1)}, s32[1,1,100]{2,1,0:T(1,128)}, u32[]{:S(2)}) copy-start(s32[1,1,100]{2,1,0:T(1,128)} %param.13) | copy-start | bytes 1204

commit v3 on v2

--- a/solution.py
+++ b/solution.py
@@ -269,15 +269,14 @@
 
 
 def spread_kernel(
-    own, other, lifts, hop_own, transit, out, hop_out, turned_rows, work, carried, sems
+    own, other, lifts, hop_own, transit, out, hop_out, turned_rows, work, sem
 ):
     core = lax.rem(lax.axis_index("band"), 2)
     far_rows = transit.shape[0]
-    fetch = pltpu.make_async_copy(transit, carried, sems.at[0])
-    store = pltpu.make_async_copy(
-        carried, hop_out.at[pl.ds(2 * far_rows, far_rows)], sems.at[1]
-    )
-    fetch.start()
+    carry = pltpu.make_async_copy(
+        transit, hop_out.at[pl.ds(2 * far_rows, far_rows)], sem
+    )
+    carry.start()
     for near in range(6):
         for i in range(LAT_DEV):
             if near == 0:
@@ -290,8 +289,6 @@
             flipped = jnp.concatenate([head, total - head], axis=0).T.astype(BF16)
             at = ((near // 2) * LAT_DEV + i) * 8 + (near % 2) * 4
             turned_rows[at * 32 : (at + 4) * 32, :] = flipped
-    fetch.wait()
-    store.start()
     group = (iota((32, 4 * BLOCK), 1) & (BLOCK - 1)) >> 4
     for chunk in range(5):
         part = turned_rows[chunk * 768 : (chunk + 1) * 768, :]
@@ -312,19 +309,28 @@
     for g in range(GROUPS):
         work[pl.ds(g * 16 + 15, 32, stride=64), :] = overflow
     out[...] = work[...].astype(BF16).reshape(out.shape)
-    store.wait()
+    carry.wait()
 
 
 def legendre_kernel(
-    orders_in, parts_in, legendre_in, grid_done, out, overflow,
-    orders, parts, work, gathered, legendre, order_sem, part_sem, load_sem,
+    orders_in, parts_in, legendre_in, last_in, grid_done, out, overflow,
+    orders, parts, work, gathered, legendre, last, order_sem, part_sem, load_sems,
 ):
     fetch = pltpu.make_async_copy(orders_in, orders, order_sem)
     fetch.start()
     bring = pltpu.make_async_copy(parts_in, parts, part_sem)
     bring.start()
-    load = pltpu.make_async_copy(legendre_in, legendre, load_sem)
-    load.start()
+    step = 256
+    lows = list(range(0, ORDERS, step))
+    loads = [
+        pltpu.make_async_copy(
+            legendre_in.at[pl.ds(low, step)], legendre.at[pl.ds(low, step)], load_sems.at[n]
+        )
+        for n, low in enumerate(lows)
+    ]
+    loads.append(pltpu.make_async_copy(last_in, last, load_sems.at[len(lows)]))
+    for load in loads:
+        load.start()
     fetch.wait()
     first = ORDERS - orders[lax.axis_index("band")]
     bring.wait()
@@ -343,11 +349,11 @@
             gathered[at : at + LAT_DEV, :] = total
             gathered[at + 20 : at + 20 + LAT_DEV, :] = pltpu.roll(total, 64, 1)
     right = gathered[...].astype(BF16)
-    load.wait()
-    step = 256
-    for low in range(0, ORDERS + 1, step):
-        size = min(step, ORDERS + 1 - low)
-        mixed = jnp.dot(legendre[low : low + size, :], right, preferred_element_type=F32).T
+    for load, low in zip(loads, lows + [ORDERS]):
+        load.wait()
+        size = step if low < ORDERS else 1
+        rows = legendre[low : low + size, :] if low < ORDERS else last[...]
+        mixed = jnp.dot(rows, right, preferred_element_type=F32).T
         degree = low + iota((16, size), 1)
         for r in range(2):
             picked = jnp.where(
@@ -531,8 +537,7 @@
         [
             pltpu.VMEM((3840, BLOCK), BF16),
             pltpu.VMEM((CHIPS * GROUPS * 16, BLOCK), F32),
-            pltpu.VMEM((pack_rows(FAR), BLOCK), BF16),
-            pltpu.SemaphoreType.DMA((2,)),
+            pltpu.SemaphoreType.DMA,
         ],
         "vertical_solve_of_fourier",
         10**9,
@@ -552,7 +557,7 @@
     grid_adj, grid_done = grid_solve(FAR, lift, kept, pair, hop_all, passed)
     spectral, overflow = call(
         legendre_kernel,
-        [HBM, ANY, HBM, ANY],
+        [HBM, ANY, HBM, ANY, ANY],
         [VMEM, SMEM],
         [((2, LEVELS, ORDERS + 1), F32), ((1, 1), F32)],
         [
@@ -560,15 +565,16 @@
             pltpu.VMEM((CHIPS * GROUPS, 16, BLOCK), BF16),
             pltpu.VMEM((CHIPS * GROUPS * 16, BLOCK), F32),
             pltpu.VMEM((LATITUDES, BLOCK), F32),
-            pltpu.VMEM((ORDERS + 1, LATITUDES), BF16),
+            pltpu.VMEM((ORDERS, LATITUDES), BF16),
+            pltpu.VMEM((1, LATITUDES), BF16),
             pltpu.SemaphoreType.DMA,
             pltpu.SemaphoreType.DMA,
-            pltpu.SemaphoreType.DMA,
+            pltpu.SemaphoreType.DMA((6,)),
         ],
         "legendre_analysis",
         2 * 10**9,
         56,
-    )(order_pairs, parts, legendre[0].T, grid_done)
+    )(order_pairs, parts, legendre[0].T, legendre[0, :, ORDERS][None], grid_done)
 
     def wide_exchange(state):
         _, kept, pair, transit, hop = payloads(

time: 55.6 us -> 56.9 us (1.023)
  local copies, waits for them, and re-layouts: 0.63 us -> 1.95 us
  waiting for transfers between devices: 13.3 us -> 12 us
  Pallas kernels: 18.4 us -> 19.6 us
    pallas_call x1, Pallas kernels: 3.95 us -> 5.45 us  [on_device(): call(legendre_kernel, [HBM, ANY, HBM, ANY, ANY], [VMEM, SMEM], [((2, LEVE...]
    another operation x0 -> x1, local copies, waits for them, and re-layouts: none -> 1.32 us  [on_device(): legendre[0, :, ORDERS][None]]
    ppermute x1, waiting for transfers between devices: 1.3 us -> 0.01 us  [on_device(): pair = lax.ppermute(pair, 'band', SWAP)]
  transfers between devices with their start and end apart: 6 -> 6, of which waited for: 4 -> 3; matrix products, arithmetic and copies ran while one was open for 0% -> 2% of each run, Pallas kernels for 9% -> 9%
where the time goes in v3:
time: 56.9 us; the launch traced here: 56.6 us
  starting transfers between devices  21.5 us (38%)
  Pallas kernels  19.6 us (34%)
  waiting for transfers between devices  12 us (21%)
  local copies, waits for them, and re-layouts  1.95 us (3%)
  between operations  0.92 us (2%)
  loops' own time  0.62 us (1%)
    all_to_all x1, starting transfers between devices, on_device(): lax.all_to_all(message, ('band', 'lev'), split_axis=0, concat_axis=0, axi...  15.1 us
    all_to_all x1, waiting for transfers between devices, on_device(): lax.all_to_all(message, ('band', 'lev'), split_axis=0, concat_axis=0, axi...  9.85 us
    pallas_call x1, Pallas kernels, payloads(): call(functools.partial(payload_kernel, far), [HBM] * 5, [VMEM, VMEM] + [H...  6.18 us
    pallas_call x1, Pallas kernels, on_device(): call(legendre_kernel, [HBM, ANY, HBM, ANY, ANY], [VMEM, SMEM], [((2, LEVE...  5.45 us
    pallas_call x1, Pallas kernels, grid_solve(): call(functools.partial(grid_kernel, far), [VMEM] + [ANY] * 4, [HBM, VMEM]...  4.42 us
    ppermute x1, starting transfers between devices, on_device(): other = lax.ppermute(other, 'band', SWAP)  3.33 us
    pallas_call x1, Pallas kernels, on_device(): call(spread_kernel, [VMEM] * 3 + [HBM, ANY], [VMEM, HBM], [((CHIPS * GROU...  2.92 us
    ppermute x1, starting transfers between devices, on_device(): hop_all = lax.ppermute(hop_all, 'band', HOP)  2.07 us
  transfers between devices with their start and end apart: 6, of which 3 were waited for; matrix products, arithmetic and copies ran while one was open for 2% of the time, Pallas kernels for 9%

profile of v3, /device:TPU:1, one launch (start us, length us, event | category | flops | bytes accessed | tf_op | source)
XLA Modules:
  0.0 56.6 jit_solution(11210667116662248855)
XLA Ops:
  0.6 0.0 copy-start
  0.6 0.0 copy-start.1
  0.6 6.2 %payload_and_part_fourier.3 = (f32[26,64,256]{2,1,0:T(8,128)S(1)}, f32[26,64,128]{2,1,0:T(8,128)S(1)}, bf16[2576,128]{1,0:T(8,128)(2,1)S(1)}, bf16[2576,128]{1,0...) custom-call(s32[100]{0:T(128)} %bitcast.17, s32[100]{0:T(128)} %bitcast.19, ...), custom_call_target="tpu_custom_call" | custom-call | flops 3000000000 | bytes 4194304 | tf_op jit(solution)/shard_map/payload_and_part_fourier/pallas_call | solution.py:448
  6.8 3.3 %collective-permute-start.4 = (f32[26,64,128]{2,1,0:T(8,128)S(1)}, f32[26,64,128]{2,1,0:T(8,128)S(1)}, u32[]{:S(2)}, u32[]{:S(2)}) collective-permute-start(f32[26,64,128]{2,1,0:T(8,128)S(1)} %get-tuple-element.67), channel_id=1, source_target_pairs={{0,4},{4,0},{8,12},{12,8},{16,20},{20,16},{24,28},{28,24},{32,36},... | collective-permute-start | bytes 2555912 | tf_op jit(solution)/shard_map/ppermute | solution.py:512
  10.2 0.1 collective-permute-start.5
  10.3 0.7 %inverse_of_vertical_operator.1 = (bf16[256,512]{1,0:T(8,128)(2,1)S(1)}, bf16[64,128]{1,0:T(8,128)(2,1)S(1)}, f32[26,64,128]{2,1,0:T(8,128)S(1)}) custom-call(f32[4,16]{1,0:T(4,128)S(1)} %copy-done, f32[4,16]{1,0:T(4,128)S(1)} %copy-done.1, f32[26,64,256]{2,1,0:T(8,128)S(1)} %get-tuple-element.65.sums), custom_call_target="tpu_custom_call" | custom-call | flops 1000000000 | bytes 4194304 | tf_op jit(solution)/shard_map/inverse_of_vertical_operator/pallas_call | solution.py:514
  11.0 1.7 %collective-permute-done.5.transit = bf16[1296,128]{1,0:T(8,128)(2,1)S(1)} collective-permute-done((bf16[1296,128]{1,0:T(8,128)(2,1)S(1)}, bf16[1296,128]{1,0:T(8,128)(2,1)S(1)}, u32[]{:S(2)}, u32[]{:S(2)}) %collective-permute-start.5) | collective-permute-done | bytes 331808 | tf_op jit(solution)/shard_map/ppermute | solution.py:513
  12.7 0.0 collective-permute-done.4.other
  12.7 2.9 %vertical_solve_of_fourier.1 = (bf16[128,16,128]{2,1,0:T(8,128)(2,1)}, bf16[3888,128]{1,0:T(8,128)(2,1)S(1)}) custom-call(f32[26,64,128]{2,1,0:T(8,128)S(1)} %get-tuple-element.66.own, f32[26,64,128]{2,1,0:T(8,128)S(1)} %collective-permute-done.4.other, bf16[256,512]{1,0:T(8,128)(2,1)S(1)} %get-tuple-element.68.lifts, ...), custom_call_target="tpu_custom_call", output_to_operand_aliasing={{1}: (3, {})} | custom-call | flops 1000000000 | bytes 4194304 | tf_op jit(solution)/shard_map/vertical_solve_of_fourier/pallas_call | solution.py:532
  15.6 2.1 %collective-permute-start.7 = (bf16[3888,128]{1,0:T(8,128)(2,1)S(1)}, bf16[3888,128]{1,0:T(8,128)(2,1)S(1)}, u32[]{:S(2)}, u32[]{:S(2)}) collective-permute-start(bf16[3888,128]{1,0:T(8,128)(2,1)S(1)} %get-tuple-element.78), channel_id=1, source_target_pairs={{4,8},{12,16},{20,24},{28,32},{36,40},{44,48},{52,56},{60,64},{68,... | collective-permute-start | bytes 2985992 | tf_op jit(solution)/shard_map/ppermute | solution.py:547
  17.7 15.1 %all-to-all-start = ((bf16[128,16,128]{2,1,0:T(8,128)(2,1)}), bf16[128,16,128]{2,1,0:T(8,128)(2,1)}, u32[]{:S(2)}, u32[]{:S(2)}) async-start(bf16[128,16,128]{2,1,0:T(8,128)(2,1)} %get-tuple-element.74), calls=%async_computation | async-start | bytes 1048576 | tf_op jit(solution)/shard_map/all_to_all | solution.py:553
  32.8 0.1 collective-permute-start.6
  32.9 0.0 collective-permute-done.7.hop_in
  33.0 0.8 %collective-permute-start.8 = (bf16[1296,128]{1,0:T(8,128)(2,1)S(1)}, bf16[1296,128]{1,0:T(8,128)(2,1)S(1)}, u32[]{:S(2)}, u32[]{:S(2)}) collective-permute-start(bf16[1296,128]{1,0:T(8,128)(2,1)S(1)} %slice.15), channel_id=1, source_target_pairs={{0,4},{4,0},{8,12},{12,8},{16,20},{20,16},{24,28},{28,24},{32,36},... | collective-permute-start | bytes 995336 | tf_op jit(solution)/shard_map/ppermute | solution.py:556
  33.7 1.3 %slice_bitcast_fusion.last_in = bf16[1,1280]{1,0:T(2,128)(2,1)} fusion(bf16[1,1280,1281]{1,2,0:T(8,128)(2,1)} %param.17), kind=kLoop, calls=%fused_computation.1 | loop fusion | bytes 5120 | tf_op jit(solution)/shard_map/broadcast_in_dim;squeeze | solution.py:577
  35.0 0.0 collective-permute-done.6.pair_in
  35.0 0.4 collective-permute-done.8.passed
  35.5 4.4 %grid_vertical_solve.3 = (f32[4,5,16,2560]{3,2,1,0:T(8,128)}, f32[8,128]{1,0:T(8,128)S(1)}) custom-call(bf16[64,128]{1,0:T(8,128)(2,1)S(1)} %get-tuple-element.115.lift, bf16[2576,128]{1,0:T(8,128)(2,1)S(1)} %get-tuple-element.76.kept, bf16[2576,128]{1,0:T(8,128)(2,1)S(1)} %collective-permute-done.6.pair_in, ...), custom_call_target="tpu_custom_call" | custom-call | flops 2000000000 | bytes 4194304 | tf_op jit(solution)/shard_map/grid_vertical_solve/pallas_call | solution.py:478
  39.9 0.0 copy-start.4
  39.9 0.6 %copy-done.4 = f32[8,128]{1,0:T(8,128)} copy-done((f32[8,128]{1,0:T(8,128)}, f32[8,128]{1,0:T(8,128)S(1)}, u32[]{:S(2)}) %copy-start.4) | copy-done | bytes 4120
  40.5 9.8 %all-to-all-done.parts_in = bf16[128,16,128]{2,1,0:T(8,128)(2,1)} async-done(((bf16[128,16,128]{2,1,0:T(8,128)(2,1)}), bf16[128,16,128]{2,1,0:T(8,128)(2,1)}, u32[]{:S(2)}, u32[]{:S(2)}) %all-to-all-start) | async-done | bytes 524320 | tf_op jit(solution)/shard_map/all_to_all | solution.py:553
  50.3 0.0 copy-done.5
  50.4 5.5 %legendre_analysis.1 = (f32[2,16,1281]{2,1,0:T(8,128)}, f32[1,1]{1,0:T(1,128)}) custom-call(s32[64]{0:T(128)S(1)} %copy-done.5, bf16[128,16,128]{2,1,0:T(8,128)(2,1)} %all-to-all-done.parts_in, bf16[1281,1280]{1,0:T(8,128)(2,1)} %bitcast.14, bf16[1,1280]{1,0:T(2,128)(2,1)} %slice_bitcast_fusion.last_in, f32[8,128]{1,0:T(8,128)} %copy-done.4), custom_call_target="tpu_custom_call" | custom-call | flops 2000000000 | bytes 4194304 | tf_op jit(solution)/shard_map/legendre_analysis/pallas_call | solution.py:558
  55.8 0.6 %while.9 = (f32[]{:T(128)}, f32[4,5,16,2560]{3,2,1,0:T(8,128)}, s32[100]{0:T(128)S(1)}, s32[100]{0:T(128)S(1)}, s32[64]{0:T(128)S(1)}, /*index=5*/bf16[4,5,16,25...) while((f32[]{:T(128)}, f32[4,5,16,2560]{3,2,1,0:T(8,128)}, s32[100]{0:T(128)S(1)}, ...), condition=%region_1.0_spmd, body=%region_0.0_spmd | while | flops 5003956736 | bytes 37404968 | solution.py:589
  (8 shorter events, 0.0 us)
Async XLA Ops:
  0.6 9.6 %copy-start = (f32[4,16]{1,0:T(4,128)S(1)}, f32[4,16]{1,0:T(4,128)}, u32[]{:S(2)}) copy-start(f32[4,16]{1,0:T(4,128)} %lower_in.1) | copy-start | bytes 772
  0.6 9.6 %copy-start.1 = (f32[4,16]{1,0:T(4,128)S(1)}, f32[4,16]{1,0:T(4,128)}, u32[]{:S(2)}) copy-start(f32[4,16]{1,0:T(4,128)} %upper_in.1) | copy-start | bytes 772
  6.8 5.8 %collective-permute-start.4 = (f32[26,64,128]{2,1,0:T(8,128)S(1)}, f32[26,64,128]{2,1,0:T(8,128)S(1)}, u32[]{:S(2)}, u32[]{:S(2)}) collective-permute-start(f32[26,64,128]{2,1,0:T(8,128)S(1)} %get-tuple-element.67), channel_id=1, source_target_pairs={{0,4},{4,0},{8,12},{12,8},{16,20},{20,16},{24,28},{28,24},{32,36},... | collective-permute-start | bytes 2555912 | tf_op jit(solution)/shard_map/ppermute | solution.py:512
  10.2 2.5 %collective-permute-start.5 = (bf16[1296,128]{1,0:T(8,128)(2,1)S(1)}, bf16[1296,128]{1,0:T(8,128)(2,1)S(1)}, u32[]{:S(2)}, u32[]{:S(2)}) collective-permute-start(bf16[1296,128]{1,0:T(8,128)(2,1)S(1)} %get-tuple-element.70), channel_id=1, source_target_pairs={{0,4},{4,0},{8,12},{12,8},{16,20},{20,16},{24,28},{28,24},{32,36},... | collective-permute-start | bytes 995336 | tf_op jit(solution)/shard_map/ppermute | solution.py:513
  15.6 17.3 %collective-permute-start.7 = (bf16[3888,128]{1,0:T(8,128)(2,1)S(1)}, bf16[3888,128]{1,0:T(8,128)(2,1)S(1)}, u32[]{:S(2)}, u32[]{:S(2)}) collective-permute-start(bf16[3888,128]{1,0:T(8,128)(2,1)S(1)} %get-tuple-element.78), channel_id=1, source_target_pairs={{4,8},{12,16},{20,24},{28,32},{36,40},{44,48},{52,56},{60,64},{68,... | collective-permute-start | bytes 2985992 | tf_op jit(solution)/shard_map/ppermute | solution.py:547
  17.7 32.7 %all-to-all-start = ((bf16[128,16,128]{2,1,0:T(8,128)(2,1)}), bf16[128,16,128]{2,1,0:T(8,128)(2,1)}, u32[]{:S(2)}, u32[]{:S(2)}) async-start(bf16[128,16,128]{2,1,0:T(8,128)(2,1)} %get-tuple-element.74), calls=%async_computation | async-start | bytes 1048576 | tf_op jit(solution)/shard_map/all_to_all | solution.py:553
  32.8 2.2 %collective-permute-start.6 = (bf16[2576,128]{1,0:T(8,128)(2,1)S(1)}, bf16[2576,128]{1,0:T(8,128)(2,1)S(1)}, u32[]{:S(2)}, u32[]{:S(2)}) collective-permute-start(bf16[2576,128]{1,0:T(8,128)(2,1)S(1)} %get-tuple-element.77), channel_id=1, source_target_pairs={{0,4},{4,0},{8,12},{12,8},{16,20},{20,16},{24,28},{28,24},{32,36},... | collective-permute-start | bytes 1978376 | tf_op jit(solution)/shard_map/ppermute | solution.py:548
  33.0 2.5 %collective-permute-start.8 = (bf16[1296,128]{1,0:T(8,128)(2,1)S(1)}, bf16[1296,128]{1,0:T(8,128)(2,1)S(1)}, u32[]{:S(2)}, u32[]{:S(2)}) collective-permute-start(bf16[1296,128]{1,0:T(8,128)(2,1)S(1)} %slice.15), channel_id=1, source_target_pairs={{0,4},{4,0},{8,12},{12,8},{16,20},{20,16},{24,28},{28,24},{32,36},... | collective-permute-start | bytes 995336 | tf_op jit(solution)/shard_map/ppermute | solution.py:556
  35.5 14.9 %copy-start.5 = (s32[64]{0:T(128)S(1)}, s32[64]{0:T(128)}, u32[]{:S(2)}) copy-start(s32[64]{0:T(128)} %orders_in.3) | copy-start | bytes 772
  39.9 0.6 %copy-start.4 = (f32[8,128]{1,0:T(8,128)}, f32[8,128]{1,0:T(8,128)S(1)}, u32[]{:S(2)}) copy-start(f32[8,128]{1,0:T(8,128)S(1)} %get-tuple-element.79.grid_done) | copy-start | bytes 12292
  50.4 5.5 %copy-start.6 = (s32[1,1,100]{2,1,0:T(1,128)S(1)}, s32[1,1,100]{2,1,0:T(1,128)}, u32[]{:S(2)}) copy-start(s32[1,1,100]{2,1,0:T(1,128)} %param.12) | copy-start | bytes 1204
  50.4 5.5 %copy-start.7 = (s32[1,1,100]{2,1,0:T(1,128)S(1)}, s32[1,1,100]{2,1,0:T(1,128)}, u32[]{:S(2)}) copy-start(s32[1,1,100]{2,1,0:T(1,128)} %param.13) | copy-start | bytes 1204

commit v4 on v2

--- a/solution.py
+++ b/solution.py
@@ -269,15 +269,14 @@
 
 
 def spread_kernel(
-    own, other, lifts, hop_own, transit, out, hop_out, turned_rows, work, carried, sems
+    own, other, lifts, hop_own, transit, out, hop_out, turned_rows, work, sem
 ):
     core = lax.rem(lax.axis_index("band"), 2)
     far_rows = transit.shape[0]
-    fetch = pltpu.make_async_copy(transit, carried, sems.at[0])
-    store = pltpu.make_async_copy(
-        carried, hop_out.at[pl.ds(2 * far_rows, far_rows)], sems.at[1]
-    )
-    fetch.start()
+    carry = pltpu.make_async_copy(
+        transit, hop_out.at[pl.ds(2 * far_rows, far_rows)], sem
+    )
+    carry.start()
     for near in range(6):
         for i in range(LAT_DEV):
             if near == 0:
@@ -290,8 +289,6 @@
             flipped = jnp.concatenate([head, total - head], axis=0).T.astype(BF16)
             at = ((near // 2) * LAT_DEV + i) * 8 + (near % 2) * 4
             turned_rows[at * 32 : (at + 4) * 32, :] = flipped
-    fetch.wait()
-    store.start()
     group = (iota((32, 4 * BLOCK), 1) & (BLOCK - 1)) >> 4
     for chunk in range(5):
         part = turned_rows[chunk * 768 : (chunk + 1) * 768, :]
@@ -312,7 +309,7 @@
     for g in range(GROUPS):
         work[pl.ds(g * 16 + 15, 32, stride=64), :] = overflow
     out[...] = work[...].astype(BF16).reshape(out.shape)
-    store.wait()
+    carry.wait()
 
 
 def legendre_kernel(
@@ -531,8 +528,7 @@
         [
             pltpu.VMEM((3840, BLOCK), BF16),
             pltpu.VMEM((CHIPS * GROUPS * 16, BLOCK), F32),
-            pltpu.VMEM((pack_rows(FAR), BLOCK), BF16),
-            pltpu.SemaphoreType.DMA((2,)),
+            pltpu.SemaphoreType.DMA,
         ],
         "vertical_solve_of_fourier",
         10**9,

time: 55.6 us -> 55.4 us (level)
  no operation moved by 1% of the time
where the time goes in v4:
time: 55.4 us; the launch traced here: 55.1 us
  starting transfers between devices  21.5 us (39%)
  Pallas kernels  18.1 us (33%)
  waiting for transfers between devices  13.3 us (24%)
  between operations  0.92 us (2%)
  local copies, waits for them, and re-layouts  0.63 us (1%)
  loops' own time  0.62 us (1%)
    all_to_all x1, starting transfers between devices, on_device(): lax.all_to_all(message, ('band', 'lev'), split_axis=0, concat_axis=0, axi...  15.2 us
    all_to_all x1, waiting for transfers between devices, on_device(): lax.all_to_all(message, ('band', 'lev'), split_axis=0, concat_axis=0, axi...  9.82 us
    pallas_call x1, Pallas kernels, payloads(): call(functools.partial(payload_kernel, far), [HBM] * 5, [VMEM, VMEM] + [H...  6.18 us
    pallas_call x1, Pallas kernels, grid_solve(): call(functools.partial(grid_kernel, far), [VMEM] + [ANY] * 4, [HBM, VMEM]...  4.42 us
    pallas_call x1, Pallas kernels, on_device(): call(legendre_kernel, [HBM, ANY, HBM, ANY], [VMEM, SMEM], [((2, LEVELS, O...  3.95 us
    ppermute x1, starting transfers between devices, on_device(): other = lax.ppermute(other, 'band', SWAP)  3.33 us
    pallas_call x1, Pallas kernels, on_device(): call(spread_kernel, [VMEM] * 3 + [HBM, ANY], [VMEM, HBM], [((CHIPS * GROU...  2.92 us
    ppermute x1, starting transfers between devices, on_device(): hop_all = lax.ppermute(hop_all, 'band', HOP)  2.07 us
  transfers between devices with their start and end apart: 6, of which 4 were waited for; matrix products, arithmetic and copies ran while one was open for 0% of the time, Pallas kernels for 9%

profile of v4, /device:TPU:1, one launch (start us, length us, event | category | flops | bytes accessed | tf_op | source)
XLA Modules:
  0.0 55.1 jit_solution(18167731438259551584)
XLA Ops:
  0.6 0.0 copy-start
  0.6 0.0 copy-start.1
  0.6 6.2 %payload_and_part_fourier.3 = (f32[26,64,256]{2,1,0:T(8,128)S(1)}, f32[26,64,128]{2,1,0:T(8,128)S(1)}, bf16[2576,128]{1,0:T(8,128)(2,1)S(1)}, bf16[2576,128]{1,0...) custom-call(s32[100]{0:T(128)} %bitcast.15, s32[100]{0:T(128)} %bitcast.17, ...), custom_call_target="tpu_custom_call" | custom-call | flops 3000000000 | bytes 4194304 | tf_op jit(solution)/shard_map/payload_and_part_fourier/pallas_call | solution.py:439
  6.8 3.3 %collective-permute-start.4 = (f32[26,64,128]{2,1,0:T(8,128)S(1)}, f32[26,64,128]{2,1,0:T(8,128)S(1)}, u32[]{:S(2)}, u32[]{:S(2)}) collective-permute-start(f32[26,64,128]{2,1,0:T(8,128)S(1)} %get-tuple-element.67), channel_id=1, source_target_pairs={{0,4},{4,0},{8,12},{12,8},{16,20},{20,16},{24,28},{28,24},{32,36},... | collective-permute-start | bytes 2555912 | tf_op jit(solution)/shard_map/ppermute | solution.py:503
  10.2 0.1 collective-permute-start.5
  10.3 0.0 copy-done
  10.3 0.0 copy-done.1
  10.3 0.7 %inverse_of_vertical_operator.1 = (bf16[256,512]{1,0:T(8,128)(2,1)S(1)}, bf16[64,128]{1,0:T(8,128)(2,1)S(1)}, f32[26,64,128]{2,1,0:T(8,128)S(1)}) custom-call(f32[4,16]{1,0:T(4,128)S(1)} %copy-done, f32[4,16]{1,0:T(4,128)S(1)} %copy-done.1, f32[26,64,256]{2,1,0:T(8,128)S(1)} %get-tuple-element.65.sums), custom_call_target="tpu_custom_call" | custom-call | flops 1000000000 | bytes 4194304 | tf_op jit(solution)/shard_map/inverse_of_vertical_operator/pallas_call | solution.py:505
  10.9 1.7 %collective-permute-done.5.transit = bf16[1296,128]{1,0:T(8,128)(2,1)S(1)} collective-permute-done((bf16[1296,128]{1,0:T(8,128)(2,1)S(1)}, bf16[1296,128]{1,0:T(8,128)(2,1)S(1)}, u32[]{:S(2)}, u32[]{:S(2)}) %collective-permute-start.5) | collective-permute-done | bytes 331808 | tf_op jit(solution)/shard_map/ppermute | solution.py:504
  12.6 0.0 collective-permute-done.4.other
  12.7 2.9 %vertical_solve_of_fourier.1 = (bf16[128,16,128]{2,1,0:T(8,128)(2,1)}, bf16[3888,128]{1,0:T(8,128)(2,1)S(1)}) custom-call(f32[26,64,128]{2,1,0:T(8,128)S(1)} %get-tuple-element.66.own, f32[26,64,128]{2,1,0:T(8,128)S(1)} %collective-permute-done.4.other, bf16[256,512]{1,0:T(8,128)(2,1)S(1)} %get-tuple-element.68.lifts, ...), custom_call_target="tpu_custom_call", output_to_operand_aliasing={{1}: (3, {})} | custom-call | flops 1000000000 | bytes 4194304 | tf_op jit(solution)/shard_map/vertical_solve_of_fourier/pallas_call | solution.py:523
  15.6 2.1 %collective-permute-start.7 = (bf16[3888,128]{1,0:T(8,128)(2,1)S(1)}, bf16[3888,128]{1,0:T(8,128)(2,1)S(1)}, u32[]{:S(2)}, u32[]{:S(2)}) collective-permute-start(bf16[3888,128]{1,0:T(8,128)(2,1)S(1)} %get-tuple-element.78), channel_id=1, source_target_pairs={{4,8},{12,16},{20,24},{28,32},{36,40},{44,48},{52,56},{60,64},{68,... | collective-permute-start | bytes 2985992 | tf_op jit(solution)/shard_map/ppermute | solution.py:538
  17.7 15.2 %all-to-all-start = ((bf16[128,16,128]{2,1,0:T(8,128)(2,1)}), bf16[128,16,128]{2,1,0:T(8,128)(2,1)}, u32[]{:S(2)}, u32[]{:S(2)}) async-start(bf16[128,16,128]{2,1,0:T(8,128)(2,1)} %get-tuple-element.74), calls=%async_computation | async-start | bytes 1048576 | tf_op jit(solution)/shard_map/all_to_all | solution.py:544
  32.8 0.1 collective-permute-start.6
  32.9 0.0 collective-permute-done.7.hop_in
  33.0 0.8 %collective-permute-start.8 = (bf16[1296,128]{1,0:T(8,128)(2,1)S(1)}, bf16[1296,128]{1,0:T(8,128)(2,1)S(1)}, u32[]{:S(2)}, u32[]{:S(2)}) collective-permute-start(bf16[1296,128]{1,0:T(8,128)(2,1)S(1)} %slice.11), channel_id=1, source_target_pairs={{0,4},{4,0},{8,12},{12,8},{16,20},{20,16},{24,28},{28,24},{32,36},... | collective-permute-start | bytes 995336 | tf_op jit(solution)/shard_map/ppermute | solution.py:547
  33.7 1.3 %collective-permute-done.6.pair_in = bf16[2576,128]{1,0:T(8,128)(2,1)S(1)} collective-permute-done((bf16[2576,128]{1,0:T(8,128)(2,1)S(1)}, bf16[2576,128]{1,0:T(8,128)(2,1)S(1)}, u32[]{:S(2)}, u32[]{:S(2)}) %collective-permute-start.6) | collective-permute-done | bytes 659488 | tf_op jit(solution)/shard_map/ppermute | solution.py:539
  35.0 0.5 collective-permute-done.8.passed
  35.5 4.4 %grid_vertical_solve.3 = (f32[4,5,16,2560]{3,2,1,0:T(8,128)}, f32[8,128]{1,0:T(8,128)S(1)}) custom-call(bf16[64,128]{1,0:T(8,128)(2,1)S(1)} %get-tuple-element.115.lift, bf16[2576,128]{1,0:T(8,128)(2,1)S(1)} %get-tuple-element.76.kept, bf16[2576,128]{1,0:T(8,128)(2,1)S(1)} %collective-permute-done.6.pair_in, ...), custom_call_target="tpu_custom_call" | custom-call | flops 2000000000 | bytes 4194304 | tf_op jit(solution)/shard_map/grid_vertical_solve/pallas_call | solution.py:469
  39.9 0.0 copy-start.4
  39.9 0.6 %copy-done.4 = f32[8,128]{1,0:T(8,128)} copy-done((f32[8,128]{1,0:T(8,128)}, f32[8,128]{1,0:T(8,128)S(1)}, u32[]{:S(2)}) %copy-start.4) | copy-done | bytes 4120
  40.5 9.8 %all-to-all-done.parts_in = bf16[128,16,128]{2,1,0:T(8,128)(2,1)} async-done(((bf16[128,16,128]{2,1,0:T(8,128)(2,1)}), bf16[128,16,128]{2,1,0:T(8,128)(2,1)}, u32[]{:S(2)}, u32[]{:S(2)}) %all-to-all-start) | async-done | bytes 524320 | tf_op jit(solution)/shard_map/all_to_all | solution.py:544
  50.3 4.0 %legendre_analysis.1 = (f32[2,16,1281]{2,1,0:T(8,128)}, f32[1,1]{1,0:T(1,128)}) custom-call(s32[64]{0:T(128)S(1)} %copy-done.5, bf16[128,16,128]{2,1,0:T(8,128)(2,1)} %all-to-all-done.parts_in, bf16[1281,1280]{1,0:T(8,128)(2,1)} %bitcast.12, f32[8,128]{1,0:T(8,128)} %copy-done.4), custom_call_target="tpu_custom_call" | custom-call | flops 2000000000 | bytes 4194304 | tf_op jit(solution)/shard_map/legendre_analysis/pallas_call | solution.py:549
  54.3 0.6 %while.9 = (f32[]{:T(128)}, f32[4,5,16,2560]{3,2,1,0:T(8,128)}, s32[100]{0:T(128)S(1)}, s32[100]{0:T(128)S(1)}, s32[64]{0:T(128)S(1)}, /*index=5*/bf16[4,5,16,25...) while((f32[]{:T(128)}, f32[4,5,16,2560]{3,2,1,0:T(8,128)}, s32[100]{0:T(128)S(1)}, ...), condition=%region_1.0_spmd, body=%region_0.0_spmd | while | flops 5003956736 | bytes 37404968 | solution.py:579
  (7 shorter events, 0.0 us)
Async XLA Ops:
  0.6 9.6 %copy-start = (f32[4,16]{1,0:T(4,128)S(1)}, f32[4,16]{1,0:T(4,128)}, u32[]{:S(2)}) copy-start(f32[4,16]{1,0:T(4,128)} %lower_in.1) | copy-start | bytes 772
  0.6 9.6 %copy-start.1 = (f32[4,16]{1,0:T(4,128)S(1)}, f32[4,16]{1,0:T(4,128)}, u32[]{:S(2)}) copy-start(f32[4,16]{1,0:T(4,128)} %upper_in.1) | copy-start | bytes 772
  6.8 5.8 %collective-permute-start.4 = (f32[26,64,128]{2,1,0:T(8,128)S(1)}, f32[26,64,128]{2,1,0:T(8,128)S(1)}, u32[]{:S(2)}, u32[]{:S(2)}) collective-permute-start(f32[26,64,128]{2,1,0:T(8,128)S(1)} %get-tuple-element.67), channel_id=1, source_target_pairs={{0,4},{4,0},{8,12},{12,8},{16,20},{20,16},{24,28},{28,24},{32,36},... | collective-permute-start | bytes 2555912 | tf_op jit(solution)/shard_map/ppermute | solution.py:503
  10.2 2.5 %collective-permute-start.5 = (bf16[1296,128]{1,0:T(8,128)(2,1)S(1)}, bf16[1296,128]{1,0:T(8,128)(2,1)S(1)}, u32[]{:S(2)}, u32[]{:S(2)}) collective-permute-start(bf16[1296,128]{1,0:T(8,128)(2,1)S(1)} %get-tuple-element.70), channel_id=1, source_target_pairs={{0,4},{4,0},{8,12},{12,8},{16,20},{20,16},{24,28},{28,24},{32,36},... | collective-permute-start | bytes 995336 | tf_op jit(solution)/shard_map/ppermute | solution.py:504
  15.6 17.3 %collective-permute-start.7 = (bf16[3888,128]{1,0:T(8,128)(2,1)S(1)}, bf16[3888,128]{1,0:T(8,128)(2,1)S(1)}, u32[]{:S(2)}, u32[]{:S(2)}) collective-permute-start(bf16[3888,128]{1,0:T(8,128)(2,1)S(1)} %get-tuple-element.78), channel_id=1, source_target_pairs={{4,8},{12,16},{20,24},{28,32},{36,40},{44,48},{52,56},{60,64},{68,... | collective-permute-start | bytes 2985992 | tf_op jit(solution)/shard_map/ppermute | solution.py:538
  17.7 32.7 %all-to-all-start = ((bf16[128,16,128]{2,1,0:T(8,128)(2,1)}), bf16[128,16,128]{2,1,0:T(8,128)(2,1)}, u32[]{:S(2)}, u32[]{:S(2)}) async-start(bf16[128,16,128]{2,1,0:T(8,128)(2,1)} %get-tuple-element.74), calls=%async_computation | async-start | bytes 1048576 | tf_op jit(solution)/shard_map/all_to_all | solution.py:544
  32.8 2.2 %collective-permute-start.6 = (bf16[2576,128]{1,0:T(8,128)(2,1)S(1)}, bf16[2576,128]{1,0:T(8,128)(2,1)S(1)}, u32[]{:S(2)}, u32[]{:S(2)}) collective-permute-start(bf16[2576,128]{1,0:T(8,128)(2,1)S(1)} %get-tuple-element.77), channel_id=1, source_target_pairs={{0,4},{4,0},{8,12},{12,8},{16,20},{20,16},{24,28},{28,24},{32,36},... | collective-permute-start | bytes 1978376 | tf_op jit(solution)/shard_map/ppermute | solution.py:539
  33.0 2.5 %collective-permute-start.8 = (bf16[1296,128]{1,0:T(8,128)(2,1)S(1)}, bf16[1296,128]{1,0:T(8,128)(2,1)S(1)}, u32[]{:S(2)}, u32[]{:S(2)}) collective-permute-start(bf16[1296,128]{1,0:T(8,128)(2,1)S(1)} %slice.11), channel_id=1, source_target_pairs={{0,4},{4,0},{8,12},{12,8},{16,20},{20,16},{24,28},{28,24},{32,36},... | collective-permute-start | bytes 995336 | tf_op jit(solution)/shard_map/ppermute | solution.py:547
  35.5 14.8 %copy-start.5 = (s32[64]{0:T(128)S(1)}, s32[64]{0:T(128)}, u32[]{:S(2)}) copy-start(s32[64]{0:T(128)} %orders_in.3) | copy-start | bytes 772
  39.9 0.6 %copy-start.4 = (f32[8,128]{1,0:T(8,128)}, f32[8,128]{1,0:T(8,128)S(1)}, u32[]{:S(2)}) copy-start(f32[8,128]{1,0:T(8,128)S(1)} %get-tuple-element.79.grid_done) | copy-start | bytes 12292
  50.3 4.0 %copy-start.6 = (s32[1,1,100]{2,1,0:T(1,128)S(1)}, s32[1,1,100]{2,1,0:T(1,128)}, u32[]{:S(2)}) copy-start(s32[1,1,100]{2,1,0:T(1,128)} %param.12) | copy-start | bytes 1204
  50.3 4.0 %copy-start.7 = (s32[1,1,100]{2,1,0:T(1,128)S(1)}, s32[1,1,100]{2,1,0:T(1,128)}, u32[]{:S(2)}) copy-start(s32[1,1,100]{2,1,0:T(1,128)} %param.13) | copy-start | bytes 1204
